TPU v7x, 256 devices: a whole 4x4x8 slice. The times are simulated.
256 devices in a mesh: dp: 32 (over x, z), ctx: 8 (over y, core).
Axes of the slice: x: 4, y: 4, z: 8, core: 2. Of those that a mesh axis runs over, the one named last changes fastest.
Arguments:
- normed_input: bfloat16 [32, 1024, 5120], P('dp', 'ctx'), may hold values from -6 to 6
- queries: bfloat16 [32, 1024, 8192], P('dp', 'ctx'), may hold values from -150 to 150
- keys: bfloat16 [32, 1024, 1024], P('dp', 'ctx'), may hold values from -6 to 6
- values: bfloat16 [32, 1024, 1024], P('dp', 'ctx'), may hold values from -6 to 6
- out_grad: bfloat16 [32, 1024, 8192], P('dp', 'ctx'), may hold values from -6 to 6
- loss_weight: int32 [32, 1024], P('dp', 'ctx'), may hold values from 0 to 3
- doc_ids: int32 [32, 1024], P('dp', 'ctx'), may hold values from 0 to 3, never falling along the last dimension, each value on 1 to 512 neighbouring positions
- adapter: float32 [64, 19456], P(None, 'dp'), may hold values from -0.078125 to 0.078125
- moment1: float32 [64, 19456], P(None, 'dp'), may hold values from -4 to 4
- moment2: float32 [64, 19456], P(None, 'dp'), may hold values from 0.05 to 1
Outputs:
- new_moment1: float32 [64, 19456], P(None, 'dp')
- new_moment2: float32 [64, 19456], P(None, 'dp')
- adam_step: float32 [64, 19456], P(None, 'dp')
Inputs may be any that keep to these rules, and one draw needn't show every extreme that they name: `doc_ids`: within a sequence document ids never fall; each document is whole and one has exactly 512 positions.
All inputs are finite; a program needn't handle non-finite values.
Results may differ from a plain program's by a relative error of at most 0.0094.
Values may be sent and summed in bfloat16 or wider, within the bound.
A program may use at most 128 MiB of HBM per device.

v0:
```python
import jax
import jax.numpy as jnp
from jax import lax
from jax.sharding import PartitionSpec as P

HEAD_SIZE = 128


THETA = 1000000.0
ADAPTER_SCALE = 2.0
BETA_ONE = 0.9
BETA_TWO = 0.95
ADAM_EPS = 1e-08
STEP_COUNT = 10


def head_backward(query_h, key_g, value_g, cot_h, docs_q, docs_k):
    rows, width = query_h.shape
    key_len = key_g.shape[0]
    block = min(rows, 512)
    scale = 1.0 / width**0.5
    key_pos = jnp.arange(key_len, dtype=jnp.int32)

    def one_block(acc, index):
        start = index * block
        q_rows = lax.dynamic_slice_in_dim(query_h, start, block, 0)
        g_rows = lax.dynamic_slice_in_dim(cot_h, start, block, 0)
        d_rows = lax.dynamic_slice_in_dim(docs_q, start, block, 0)
        q_pos = start + jnp.arange(block, dtype=jnp.int32)
        scores = (
            lax.dot_general(
                q_rows, key_g, (((1,), (1,)), ((), ())), preferred_element_type=jnp.float32
            )
            * scale
        )
        allowed = (key_pos[None, :] <= q_pos[:, None]) & (docs_k[None, :] == d_rows[:, None])
        scores = jnp.where(allowed, scores, -jnp.inf)
        top = jnp.max(scores, axis=1, keepdims=True)
        expo = jnp.exp(scores - top)
        probs = expo / jnp.sum(expo, axis=1, keepdims=True)
        probs_b = probs.astype(jnp.bfloat16)
        dprobs = lax.dot_general(
            g_rows, value_g, (((1,), (1,)), ((), ())), preferred_element_type=jnp.float32
        )
        delta = jnp.sum(probs * dprobs, axis=1, keepdims=True)
        dscores = (probs * (dprobs - delta) * scale).astype(jnp.bfloat16)
        dq_rows = jnp.dot(dscores, key_g, preferred_element_type=jnp.float32).astype(jnp.bfloat16)
        acc = acc + lax.dot_general(
            probs_b, g_rows, (((0,), (0,)), ((), ())), preferred_element_type=jnp.float32
        )
        return (acc, dq_rows)

    dv_acc, dq_blocks = lax.scan(
        one_block,
        jnp.zeros((key_len, width), jnp.float32),
        jnp.arange(rows // block, dtype=jnp.int32),
    )
    return (dq_blocks.reshape(rows, width), dv_acc)


def group_backward(query_g, key_g, value_g, cot_g, docs_q, docs_k):
    rows = query_g.shape[0]
    key_len, head_w = key_g.shape
    group = query_g.shape[1] // head_w
    q_heads = query_g.reshape(rows, group, head_w).transpose(1, 0, 2)
    c_heads = cot_g.reshape(rows, group, head_w).transpose(1, 0, 2)

    def one_head(acc, pair):
        dq_h, dv_h = head_backward(pair[0], key_g, value_g, pair[1], docs_q, docs_k)
        return (acc + dv_h, dq_h)

    dv_sum, dq_heads = lax.scan(
        one_head, jnp.zeros((key_len, head_w), jnp.float32), (q_heads, c_heads)
    )
    return (dq_heads.transpose(1, 0, 2).reshape(rows, group * head_w), dv_sum)


def rope_back(dq_rot, start, head_w):
    sequence_length, width = dq_rot.shape
    half = head_w // 2
    pos = start.astype(jnp.float32) + jnp.arange(sequence_length, dtype=jnp.float32)
    freq = THETA ** (-(jnp.arange(half, dtype=jnp.float32) * 2.0 / head_w))
    angle = pos[:, None] * freq[None, :]
    cosine = jnp.cos(angle)[:, None, :]
    sine = jnp.sin(angle)[:, None, :]
    upper = dq_rot.astype(jnp.float32).reshape(sequence_length, width // head_w, head_w)
    first = upper[:, :, :half]
    second = upper[:, :, half:]
    out_first = first * cosine + second * sine
    out_second = second * cosine - first * sine
    return (
        jnp.concatenate([out_first, out_second], axis=2)
        .reshape(sequence_length, width)
        .astype(jnp.bfloat16)
    )


def adapter_gradient(hidden_rows, query_gradient, dv, lowrank_factors):
    width = hidden_rows.shape[1]
    q_width = query_gradient.shape[1]
    a_query = lowrank_factors[:, :width]
    a_value = lowrank_factors[:, width : 2 * width]
    b_query = lowrank_factors[:, 2 * width : 2 * width + q_width]
    b_value = lowrank_factors[:, 2 * width + q_width :]
    inner = (((1,), (1,)), ((), ()))
    outer = (((0,), (0,)), ((), ()))
    low_q = lax.dot_general(hidden_rows, a_query, inner, preferred_element_type=jnp.float32).astype(
        jnp.bfloat16
    )
    low_v = lax.dot_general(hidden_rows, a_value, inner, preferred_element_type=jnp.float32).astype(
        jnp.bfloat16
    )
    mid_q = lax.dot_general(
        query_gradient, b_query, inner, preferred_element_type=jnp.float32
    ).astype(jnp.bfloat16)
    mid_v = lax.dot_general(dv, b_value, inner, preferred_element_type=jnp.float32).astype(
        jnp.bfloat16
    )
    grad_aq = lax.dot_general(mid_q, hidden_rows, outer, preferred_element_type=jnp.float32)
    grad_av = lax.dot_general(mid_v, hidden_rows, outer, preferred_element_type=jnp.float32)
    grad_bq = lax.dot_general(low_q, query_gradient, outer, preferred_element_type=jnp.float32)
    grad_bv = lax.dot_general(low_v, dv, outer, preferred_element_type=jnp.float32)
    return jnp.concatenate([grad_aq, grad_av, grad_bq, grad_bv], axis=1)


def adam_update(gradient_tree, moment1, moment2):
    new_m = BETA_ONE * moment1 + (1.0 - BETA_ONE) * gradient_tree
    new_v = BETA_TWO * moment2 + (1.0 - BETA_TWO) * gradient_tree * gradient_tree
    corr_one = 1.0 - BETA_ONE**STEP_COUNT
    corr_two = 1.0 - BETA_TWO**STEP_COUNT
    step = new_m / corr_one / (jnp.sqrt(new_v / corr_two) + ADAM_EPS)
    return (new_m, new_v, step)


def per_device(
    normed_input, queries, keys, values, out_grad, loss_weight, doc_ids, adapter, moment1, moment2
):
    data_parallel_count = lax.axis_size("dp")
    ctx_pos = lax.axis_index("ctx")
    tok_rows = normed_input.shape[1]
    offset = ctx_pos * tok_rows
    lowrank_factors = lax.all_gather(adapter.astype(jnp.bfloat16), "dp", axis=1, tiled=True)
    weighted_values = (out_grad * loss_weight[:, :, None].astype(jnp.float32)).astype(jnp.bfloat16)
    docs = lax.all_gather(doc_ids, "ctx", axis=1, tiled=True)[0]
    q_heads, g_heads, k_heads, v_heads = (
        lax.all_to_all(queries, "ctx", split_axis=2, concat_axis=1, tiled=True),
        lax.all_to_all(weighted_values, "ctx", split_axis=2, concat_axis=1, tiled=True),
        lax.all_to_all(keys, "ctx", split_axis=2, concat_axis=1, tiled=True),
        lax.all_to_all(values, "ctx", split_axis=2, concat_axis=1, tiled=True),
    )
    groups_here = k_heads.shape[2] // HEAD_SIZE
    q_width = q_heads.shape[2] // groups_here
    dq_g, dv_g = group_backward(
        q_heads[0, :, 0:q_width],
        k_heads[0, :, 0:HEAD_SIZE],
        v_heads[0, :, 0:HEAD_SIZE],
        g_heads[0, :, 0:q_width],
        docs,
        docs,
    )
    dv_parts = dv_g.astype(jnp.bfloat16)
    dq_rot_heads = dq_g[None]
    dv_heads = dv_parts[None]
    dq_rot_tok, dv_tok = (
        lax.all_to_all(dq_rot_heads, "ctx", split_axis=1, concat_axis=2, tiled=True),
        lax.all_to_all(dv_heads, "ctx", split_axis=1, concat_axis=2, tiled=True),
    )
    dq_rot_local = dq_rot_tok[0]
    local_value_gradient = dv_tok[0]
    query_gradient = rope_back(dq_rot_local, offset, HEAD_SIZE)
    partial_value_sum = adapter_gradient(
        normed_input[0], query_gradient, local_value_gradient, lowrank_factors
    ) * (ADAPTER_SCALE / data_parallel_count)
    shard = lax.psum_scatter(partial_value_sum, "dp", scatter_dimension=1, tiled=True)
    shard = lax.psum(shard, "ctx")
    return adam_update(shard, moment1, moment2)


def solution(mesh):
    in_specs = (
        P("dp", "ctx", None),
        P("dp", "ctx", None),
        P("dp", "ctx", None),
        P("dp", "ctx", None),
        P("dp", "ctx", None),
        P("dp", "ctx"),
        P("dp", "ctx"),
        P(None, "dp"),
        P(None, "dp"),
        P(None, "dp"),
    )
    out_specs = (P(None, "dp"), P(None, "dp"), P(None, "dp"))
    return jax.shard_map(
        per_device, mesh=mesh, in_specs=in_specs, out_specs=out_specs, check_vma=False
    )
```

profile of v0, /device:TPU:1, one launch (start us, length us, event | category | flops | bytes accessed | tf_op | source)
XLA Modules:
  0.0 855.0 jit_solution(16513180556992414151)
XLA Ops:
  12.1 6.6 all-to-all-start.2
  25.9 5.0 all-to-all-start.3
  32.9 6.9 copy.82
  39.7 45.2 %reduce.1 = bf16[8192,128]{1,0:T(8,128)(2,1)S(1)} reduce(bf16[8192,1,128]{2,1,0:T(2,128)(2,1)} %bitcast.122, bf16[]{:T(256)} %broadcast.89), dimensions={1}, to_apply=%bitcast.83.reduce_sub_computation | reduce | bytes 4194306
  88.2 16.9 %all-to-all-start.1 = ((bf16[8,2,65536]{2,1,0:T(2,128)(2,1)}), bf16[8,2,65536]{2,1,0:T(2,128)(2,1)S(1)}, u32[]{:S(2)}, u32[]{:S(2)}) async-start(bf16[8,2,65536]{2,1,0:T(2,128)(2,1)} %reshape.108), calls=%async_computation.1 | async-start | bytes 4194304 | tf_op jit(solution)/shard_map/all_to_all | solution.py:147
  105.1 9.5 %copy.80 = bf16[1,128,8192]{1,0,2:T(2,128)(2,1)} copy(bf16[1,128,8192]{2,1,0:T(8,128)(2,1)} %param.15) | data formatting | bytes 4194304 | tf_op args[1]
  114.5 46.5 %reduce = bf16[8192,128]{1,0:T(8,128)(2,1)} reduce(bf16[8192,1,128]{2,1,0:T(2,128)(2,1)} %bitcast.126, bf16[]{:T(256)} %broadcast.89), dimensions={1}, to_apply=%bitcast.81.reduce_sub_computation | reduce | bytes 4194306
  161.1 5.9 reshape.106
  167.0 4.9 all-to-all-start
  173.5 28.3 %all_gather.6 = s32[1,1024]{1,0:T(1,128)S(1)} all-gather(s32[1,128]{1,0:T(1,128)S(1)} %copy-done.10), channel_id=1, replica_groups=mesh['dp'=32,'ctx'=8] {'ctx'}, dimensions={1}, use_global_device_ids=true | all-gather | bytes 4608 | tf_op jit(solution)/shard_map/all_gather | solution.py:144
  212.7 4.4 reshape.109
  226.0 6.8 reshape.107
  241.9 184.7 %while.28 = (s32[]{:T(128)}, f32[1024,128]{1,0:T(8,128)}, bf16[8,1024,128]{1,2,0:T(8,128)(2,1)}, bf16[8,1024,128]{2,1,0:T(8,128)(2,1)}, bf16[8,1024,128]{2,1,0:T...) while((s32[]{:T(128)}, f32[1024,128]{1,0:T(8,128)}, ...), condition=%wide.region_6.7_spmd.clone, body=%wide.region_0.6_spmd.clone.sunk | while | flops 548469760 | bytes 23893576 | solution.py:72
  243.7 17.4 %while.29 = (s32[]{:T(128)}, f32[1024,128]{1,0:T(8,128)}, bf16[2,512,128]{2,1,0:T(8,128)(2,1)}, s32[2]{0:T(128)S(1)}, s32[1,1024]{1,0:T(1,128)S(1)}, /*index=5*/...) while((s32[]{:T(128)}, f32[1024,128]{1,0:T(8,128)}, ...), condition=%wide.region_5.5_spmd.clone, body=%wide.region_1.4_spmd.clone.sunk | while | flops 548207616 | bytes 20222768 | solution.py:53
  266.7 17.4 %while.29 = (s32[]{:T(128)}, f32[1024,128]{1,0:T(8,128)}, bf16[2,512,128]{2,1,0:T(8,128)(2,1)}, s32[2]{0:T(128)S(1)}, s32[1,1024]{1,0:T(1,128)S(1)}, /*index=5*/...) while((s32[]{:T(128)}, f32[1024,128]{1,0:T(8,128)}, ...), condition=%wide.region_5.5_spmd.clone, body=%wide.region_1.4_spmd.clone.sunk | while | flops 548207616 | bytes 20222768 | solution.py:53
  289.8 17.4 %while.29 = (s32[]{:T(128)}, f32[1024,128]{1,0:T(8,128)}, bf16[2,512,128]{2,1,0:T(8,128)(2,1)}, s32[2]{0:T(128)S(1)}, s32[1,1024]{1,0:T(1,128)S(1)}, /*index=5*/...) while((s32[]{:T(128)}, f32[1024,128]{1,0:T(8,128)}, ...), condition=%wide.region_5.5_spmd.clone, body=%wide.region_1.4_spmd.clone.sunk | while | flops 548207616 | bytes 20222768 | solution.py:53
  312.9 17.4 %while.29 = (s32[]{:T(128)}, f32[1024,128]{1,0:T(8,128)}, bf16[2,512,128]{2,1,0:T(8,128)(2,1)}, s32[2]{0:T(128)S(1)}, s32[1,1024]{1,0:T(1,128)S(1)}, /*index=5*/...) while((s32[]{:T(128)}, f32[1024,128]{1,0:T(8,128)}, ...), condition=%wide.region_5.5_spmd.clone, body=%wide.region_1.4_spmd.clone.sunk | while | flops 548207616 | bytes 20222768 | solution.py:53
  336.0 17.4 %while.29 = (s32[]{:T(128)}, f32[1024,128]{1,0:T(8,128)}, bf16[2,512,128]{2,1,0:T(8,128)(2,1)}, s32[2]{0:T(128)S(1)}, s32[1,1024]{1,0:T(1,128)S(1)}, /*index=5*/...) while((s32[]{:T(128)}, f32[1024,128]{1,0:T(8,128)}, ...), condition=%wide.region_5.5_spmd.clone, body=%wide.region_1.4_spmd.clone.sunk | while | flops 548207616 | bytes 20222768 | solution.py:53
  359.1 17.4 %while.29 = (s32[]{:T(128)}, f32[1024,128]{1,0:T(8,128)}, bf16[2,512,128]{2,1,0:T(8,128)(2,1)}, s32[2]{0:T(128)S(1)}, s32[1,1024]{1,0:T(1,128)S(1)}, /*index=5*/...) while((s32[]{:T(128)}, f32[1024,128]{1,0:T(8,128)}, ...), condition=%wide.region_5.5_spmd.clone, body=%wide.region_1.4_spmd.clone.sunk | while | flops 548207616 | bytes 20222768 | solution.py:53
  382.2 17.4 %while.29 = (s32[]{:T(128)}, f32[1024,128]{1,0:T(8,128)}, bf16[2,512,128]{2,1,0:T(8,128)(2,1)}, s32[2]{0:T(128)S(1)}, s32[1,1024]{1,0:T(1,128)S(1)}, /*index=5*/...) while((s32[]{:T(128)}, f32[1024,128]{1,0:T(8,128)}, ...), condition=%wide.region_5.5_spmd.clone, body=%wide.region_1.4_spmd.clone.sunk | while | flops 548207616 | bytes 20222768 | solution.py:53
  405.3 17.4 %while.29 = (s32[]{:T(128)}, f32[1024,128]{1,0:T(8,128)}, bf16[2,512,128]{2,1,0:T(8,128)(2,1)}, s32[2]{0:T(128)S(1)}, s32[1,1024]{1,0:T(1,128)S(1)}, /*index=5*/...) while((s32[]{:T(128)}, f32[1024,128]{1,0:T(8,128)}, ...), condition=%wide.region_5.5_spmd.clone, body=%wide.region_1.4_spmd.clone.sunk | while | flops 548207616 | bytes 20222768 | solution.py:53
  438.7 7.7 copy.91
  446.4 12.8 %reduce.5 = bf16[1024,1024]{1,0:T(8,128)(2,1)S(1)} reduce(bf16[1024,1,1024]{2,1,0:T(2,128)(2,1)} %bitcast.121, bf16[]{:T(256)} %broadcast.89), dimensions={1}, to_apply=%bitcast.91.reduce_sub_computation | reduce | bytes 4194306
  463.0 4.8 all-to-all-start.4
  473.5 20.7 %all-to-all-done.4 = bf16[8,2,65536]{2,1,0:T(2,128)(2,1)S(1)} async-done(((bf16[8,2,65536]{2,1,0:T(2,128)(2,1)}), bf16[8,2,65536]{2,1,0:T(2,128)(2,1)S(1)}, u32[]{:S(2)}, u32[]{:S(2)}) %all-to-all-start.4) | async-done | bytes 2097184 | tf_op jit(solution)/shard_map/all_to_all | solution.py:165
  494.2 4.4 reshape.117
  503.9 5.3 copy.93
  512.3 4.8 copy.94
  517.1 6.3 reshape.103
  540.2 8.2 copy.97
  548.5 229.9 %reduce-scatter.4.cloned.1.call-done = f32[608,64]{1,0:T(8,128)} async-done(((f32[19456,64]{1,0:T(8,128)}), f32[608,64]{1,0:T(8,128)}) %reduce-scatter.4.cloned.1.call-update) | async-done | bytes 155664
  780.1 66.2 %all-reduce.2.cloned.1.call-done = f32[64,608]{1,0:T(8,128)} async-done(((f32[64,608]{1,0:T(8,128)}), f32[64,608]{1,0:T(8,128)}) %all-reduce.2.cloned.1.call-update) | async-done | bytes 155664 | tf_op jit(solution)/shard_map/psum | solution.py:175
  (360 shorter events, 271.4 us)
Async XLA Ops:
  7.2 516.3 %copy-start = (bf16[1,128,5120]{2,1,0:T(8,128)(2,1)S(1)}, bf16[1,128,5120]{2,1,0:T(8,128)(2,1)}, u32[]{:S(2)}) copy-start(bf16[1,128,5120]{2,1,0:T(8,128)(2,1)} %param.14) | copy-start | bytes 3932164
  7.2 11.5 %copy-start.5 = (bf16[1,128,1024]{2,1,0:T(8,128)(2,1)S(1)}, bf16[1,128,1024]{2,1,0:T(8,128)(2,1)}, u32[]{:S(2)}) copy-start(bf16[1,128,1024]{2,1,0:T(8,128)(2,1)} %param.17) | copy-start | bytes 786436
  8.6 13.4 %copy-start.11 = (s32[1,128]{1,0:T(1,128)S(1)}, s32[1,128]{1,0:T(1,128)}, u32[]{:S(2)}) copy-start(s32[1,128]{1,0:T(1,128)} %param.19) | copy-start | bytes 1540
  12.1 13.1 %all-to-all-start.2 = ((bf16[8,2,8192]{2,1,0:T(2,128)(2,1)}), bf16[8,2,8192]{2,1,0:T(2,128)(2,1)S(1)}, u32[]{:S(2)}, u32[]{:S(2)}) async-start(bf16[8,2,8192]{2,1,0:T(2,128)(2,1)} %reshape.110), calls=%async_computation.2 | async-start | bytes 524288 | tf_op jit(solution)/shard_map/all_to_all | solution.py:148
  25.9 62.3 %all-to-all-start.3 = ((bf16[8,2,8192]{2,1,0:T(2,128)(2,1)}), bf16[8,2,8192]{2,1,0:T(2,128)(2,1)}, u32[]{:S(2)}, u32[]{:S(2)}) async-start(bf16[8,2,8192]{2,1,0:T(2,128)(2,1)} %reshape.112), calls=%async_computation.3 | async-start | bytes 524288 | tf_op jit(solution)/shard_map/all_to_all | solution.py:149
  88.2 78.8 %all-to-all-start.1 = ((bf16[8,2,65536]{2,1,0:T(2,128)(2,1)}), bf16[8,2,65536]{2,1,0:T(2,128)(2,1)S(1)}, u32[]{:S(2)}, u32[]{:S(2)}) async-start(bf16[8,2,65536]{2,1,0:T(2,128)(2,1)} %reshape.108), calls=%async_computation.1 | async-start | bytes 4194304 | tf_op jit(solution)/shard_map/all_to_all | solution.py:147
  166.9 6.6 copy-start.10
  167.0 59.0 %all-to-all-start = ((bf16[8,2,65536]{2,1,0:T(2,128)(2,1)}), bf16[8,2,65536]{2,1,0:T(2,128)(2,1)}, u32[]{:S(2)}, u32[]{:S(2)}) async-start(bf16[8,2,65536]{2,1,0:T(2,128)(2,1)} %reshape.106), calls=%async_computation | async-start | bytes 4194304 | tf_op jit(solution)/shard_map/all_to_all | solution.py:146
  171.9 340.4 %all-gather.3.cloned.1.call-start = ((), (), s32[]{:S(2)}) async-start(), calls=%async_computation.8 | async-start | bytes 2703360 | tf_op jit(solution)/shard_map/all_gather | solution.py:142
  245.2 2.3 copy-start.2
  245.2 2.3 copy-start.7
  253.8 2.3 copy-start.2
  253.8 2.3 copy-start.7
  276.7 2.3 copy-start.7
  291.2 2.3 copy-start.2
  291.2 2.3 copy-start.7
  322.9 2.3 copy-start.2
  322.9 2.3 copy-start.7
  360.5 2.3 copy-start.2
  360.5 2.3 copy-start.7
  369.1 2.3 copy-start.7
  392.2 2.3 copy-start.7
  406.7 2.3 copy-start.2
  406.8 2.3 copy-start.7
  426.6 12.2 %copy-start.3 = (bf16[8,1024,128]{1,2,0:T(8,128)(2,1)S(1)}, bf16[8,1024,128]{1,2,0:T(8,128)(2,1)}, u32[]{:S(2)}) copy-start(bf16[8,1024,128]{1,2,0:T(8,128)(2,1)} %get-tuple-element.109) | copy-start | bytes 6291460
  434.6 28.4 %all-to-all-start.5 = ((bf16[8,2,8192]{2,1,0:T(2,128)(2,1)}), bf16[8,2,8192]{2,1,0:T(2,128)(2,1)}, u32[]{:S(2)}, u32[]{:S(2)}) async-start(bf16[8,2,8192]{2,1,0:T(2,128)(2,1)} %reshape.114), calls=%async_computation.5 | async-start | bytes 524288 | tf_op jit(solution)/shard_map/all_to_all | solution.py:166
  463.0 31.2 %all-to-all-start.4 = ((bf16[8,2,65536]{2,1,0:T(2,128)(2,1)}), bf16[8,2,65536]{2,1,0:T(2,128)(2,1)S(1)}, u32[]{:S(2)}, u32[]{:S(2)}) async-start(bf16[8,2,65536]{2,1,0:T(2,128)(2,1)} %reshape.116), calls=%async_computation.4 | async-start | bytes 4194304 | tf_op jit(solution)/shard_map/all_to_all | solution.py:165
  467.8 310.5 %reduce-scatter.4.cloned.1.call-start = ((), (), s32[]{:S(2)}) async-start(), calls=%async_computation.9 | async-start | bytes 10272768
  530.9 5.4 copy-start.1
  548.4 298.0 %copy-start.8 = (f32[64,608]{1,0:T(8,128)S(1)}, f32[64,608]{1,0:T(8,128)}, u32[]{:S(2)}) copy-start(f32[64,608]{1,0:T(8,128)} %param.23) | copy-start | bytes 466948
  548.4 298.0 %copy-start.9 = (f32[64,608]{1,0:T(8,128)S(1)}, f32[64,608]{1,0:T(8,128)}, u32[]{:S(2)}) copy-start(f32[64,608]{1,0:T(8,128)} %param.22) | copy-start | bytes 466948
  548.4 297.9 %all-reduce.2.cloned.1.call-start = ((), (), s32[]{:S(2)}) async-start(), calls=%async_computation.7 | async-start | bytes 327680 | tf_op jit(solution)/shard_map/psum | solution.py:175
  (34 other events, 54.6 us)
Sparse Core Ops, SparseCore 0:
  175.9 77.3 all-gather.2
  548.5 229.7 reduce-scatter.3
  781.2 65.0 all-reduce.1
where the time goes:
time: 867 us; the launch traced here: 855 us
  waiting for transfers between devices  320 us (37%)
  local copies, waits for them, and re-layouts  170 us (20%)
  other arithmetic  153 us (18%)
  matrix products  116 us (13%)
  starting transfers between devices  42.3 us (5%)
  blocking collectives  28.3 us (3%)
  between operations  14.3 us (2%)
  loops' own time  11.6 us (1%)
    unnamed x4, waiting for transfers between devices  230 us
    unnamed x8, other arithmetic  114 us
    unnamed x46, local copies, waits for them, and re-layouts  84.2 us
    psum x1, waiting for transfers between devices, per_device(): shard = lax.psum(shard, 'ctx')  66.2 us
    dot_general x16, matrix products, one_block(): lax.dot_general(probs_b, g_rows, (((0,), (0,)), ((), ())), preferred_elem...  40.5 us
    dot_general x16, matrix products, one_block(): lax.dot_general(q_rows, key_g, (((1,), (1,)), ((), ())), preferred_elemen...  28.7 us
    all_gather x1, blocking collectives, per_device(): docs = lax.all_gather(doc_ids, 'ctx', axis=1, tiled=True)[0]  28.3 us
    dot_general x16, matrix products, one_block(): jnp.dot(dscores, key_g, preferred_element_type=jnp.float32)  23.4 us
  transfers between devices with their start and end apart: 9, of which 4 were waited for; matrix products, arithmetic and copies ran while one was open for 45% of the time, Pallas kernels for 0%

commit v1 on v0

v1 whole, which is shorter than its diff:
```python
import functools

import jax
import jax.numpy as jnp
import numpy as np
from jax import lax
from jax.experimental import pallas as pl
from jax.experimental.pallas import tpu as pltpu
from jax.sharding import PartitionSpec as P

HEAD = 128
GROUP = 8
KV = 8
D = 5120
RANK = 64
ROWS = 128
BLOCKS = 5
WINDOW = BLOCKS * ROWS
QW = KV * GROUP * HEAD
FACT = 2 * D + QW + KV * HEAD
BQ = 2 * D
BV = BQ + QW
NX, NZ, NY, NC = 4, 8, 4, 2
SHARD = FACT // (NX * NZ)
XCOLS = FACT // NX
HALF = XCOLS // 2
CUT = 1152
REST = HALF - CUT
WIN = 768

THETA = 1000000.0
ADAPTER_SCALE = 2.0
BETA_ONE = 0.9
BETA_TWO = 0.95
ADAM_EPS = 1e-08
STEP_COUNT = 10
NEG = -1e30
MESH = pl.DeviceIdType.MESH
NT = (((1,), (1,)), ((), ()))
NN = (((1,), (0,)), ((), ()))
F32 = jnp.float32
BF16 = jnp.bfloat16


def rope_tables():
    freq = THETA ** (-(np.arange(HEAD // 2, dtype=np.float64) * 2.0 / HEAD))
    angle = freq[:, None] * np.arange(NY * NC * ROWS, dtype=np.float64)[None, :]
    both = np.stack([np.cos(angle), np.sin(angle)])
    return both.reshape(2, HEAD // 2, NY * NC, ROWS).transpose(2, 0, 1, 3).astype(np.float32)


def dot(a, b, dims):
    return lax.dot_general(a, b, dims, preferred_element_type=F32)


def attention_kernel(
    q_ref, g_ref, lw_ref, docs_ref, k_ref, v_ref, table_ref,
    dq_ref, dv_ref,
    kv_buf, doc_buf, bias, lw_t, table, p_buf, w_buf, kt_buf,
    table_sem, doc_send, doc_recv, send_sem, recv_sem,
):
    dp = lax.axis_index("dp")
    c = lax.axis_index("ctx")
    y = c // 2
    core = c % 2

    table_copy = pltpu.make_async_copy(table_ref.at[c], table, table_sem)
    table_copy.start()

    barrier = pltpu.get_barrier_semaphore()
    for j in range(1, BLOCKS):
        @pl.when(c >= j)
        def _():
            pl.semaphore_signal(barrier, inc=1, device_id=(dp, c - j), device_id_type=MESH)

        @pl.when(c + j < 8)
        def _():
            pl.semaphore_signal(barrier, inc=1, device_id=(dp, c + j), device_id_type=MESH)

    own = BLOCKS - 1
    doc_buf[own] = jnp.broadcast_to(docs_ref[...].astype(F32), (8, ROWS))
    for h in range(KV):
        kv_buf[h, own, 0] = k_ref[:, h * HEAD:(h + 1) * HEAD]
        kv_buf[h, own, 1] = v_ref[:, h * HEAD:(h + 1) * HEAD]

    for slot in range(own):
        @pl.when(c + slot < own)
        def _():
            doc_buf[slot] = jnp.full((8, ROWS), -1.0, F32)
            for h in range(KV):
                kv_buf[h, slot] = jnp.zeros((2, ROWS, HEAD), BF16)

    pl.semaphore_wait(barrier, jnp.minimum(c, own) + jnp.minimum(7 - c, own))

    def doc_copy(j):
        return pltpu.make_async_remote_copy(
            src_ref=doc_buf.at[own], dst_ref=doc_buf.at[own - j],
            send_sem=doc_send.at[j - 1], recv_sem=doc_recv.at[own - j],
            device_id=(dp, c + j), device_id_type=MESH)

    def kv_copy(h, kind, source, target, peer):
        return pltpu.make_async_remote_copy(
            src_ref=kv_buf.at[h, source], dst_ref=kv_buf.at[h, target],
            send_sem=send_sem.at[h, kind], recv_sem=recv_sem.at[h, target],
            device_id=(dp, peer), device_id_type=MESH)

    def hop_own(h):
        return kv_copy(h, 0, 4, 2, c + 2)

    def pair_own(h):
        return kv_copy(h, 1, 4, 3, c + 1)

    def hop_relay(h):
        return kv_copy(h, 2, 2, 0, c + 2)

    def pair_near_up(h):
        return kv_copy(h, 3, 2, 1, c + 1)

    def pair_near_down(h):
        return kv_copy(h, 3, 2, 3, c - 1)

    def pair_far_down(h):
        return kv_copy(h, 4, 0, 1, c - 1)

    for j in range(1, BLOCKS):
        @pl.when(c + j < 8)
        def _():
            doc_copy(j).start()

    def send_own(h, carry):
        @pl.when(y < 3)
        def _():
            hop_own(h).start()

        @pl.when(core == 0)
        def _():
            pair_own(h).start()
        return carry

    lax.fori_loop(0, KV, send_own, 0)

    def relay_near(h):
        @pl.when(y >= 1)
        def _():
            hop_own(h).wait_recv()

            @pl.when(y < 3)
            def _():
                hop_relay(h).start()

            @pl.when(core == 0)
            def _():
                pair_near_up(h).start()

            @pl.when(core == 1)
            def _():
                pair_near_down(h).start()

    def relay_far(h):
        @pl.when(y >= 2)
        def _():
            hop_relay(h).wait_recv()

            @pl.when(core == 1)
            def _():
                pair_far_down(h).start()

    def arrive(h):
        @pl.when(jnp.logical_or(core == 1, y >= 1))
        def _():
            pair_own(h).wait_recv()

        @pl.when(jnp.logical_or(y >= 2, jnp.logical_and(core == 1, y >= 1)))
        def _():
            pair_far_down(h).wait_recv()

    lw_t[...] = jnp.broadcast_to(lw_ref[...].astype(F32), (ROWS, ROWS)).T
    table_copy.wait()
    relay_near(0)
    relay_near(1)
    for slot in range(own):
        @pl.when(c + slot >= own)
        def _():
            doc_copy(own - slot).wait_recv()
    doc_row = doc_buf[own][0:1, :]
    row_pos = lax.broadcasted_iota(jnp.int32, (ROWS, ROWS), 1)
    key_pos = lax.broadcasted_iota(jnp.int32, (ROWS, ROWS), 0)
    for slot in range(BLOCKS):
        doc_col = jnp.broadcast_to(doc_buf[slot][0:1, :], (ROWS, ROWS)).T
        allowed = doc_col == doc_row
        if slot == own:
            allowed = jnp.logical_and(allowed, key_pos <= row_pos)
        block = jnp.where(allowed, 0.0, NEG)
        bias[slot * ROWS:(slot + 1) * ROWS, 0:ROWS] = block
        bias[slot * ROWS:(slot + 1) * ROWS, ROWS:] = block
    relay_far(0)

    scale = 1.0 / HEAD ** 0.5
    fold = scale * float(np.log2(np.e))

    def one_group(h, carry):
        @pl.when(h + 2 < KV)
        def _():
            relay_near(h + 2)

        @pl.when(h + 1 < KV)
        def _():
            relay_far(h + 1)

        arrive(h)
        keys = kv_buf[h, :, 0].reshape(WINDOW, HEAD)
        vals = kv_buf[h, :, 1].reshape(WINDOW, HEAD)
        kt_buf[...] = keys.astype(F32).T.astype(BF16)
        cosine = jnp.concatenate([table[0], table[0]], axis=1)
        sine = jnp.concatenate([table[1], table[1]], axis=1)
        for pair in range(GROUP // 2):
            cols = [
                pl.ds(pl.multiple_of(h * GROUP * HEAD + (2 * pair + t) * HEAD, HEAD), HEAD)
                for t in range(2)
            ]
            q_two = jnp.concatenate([q_ref[:, cols[0]], q_ref[:, cols[1]]], axis=0)
            w_two = jnp.concatenate(
                [(g_ref[:, s].astype(F32) * lw_t[...]).astype(BF16) for s in cols], axis=0)
            w_buf[pair * 256:(pair + 1) * 256, :] = w_two
            scores = dot(keys, q_two, NT) + bias[...]
            top = jnp.max(scores, axis=0, keepdims=True)
            expo = jnp.exp2((scores - top) * fold)
            probs = expo * (1.0 / jnp.sum(expo, axis=0, keepdims=True))
            dprobs = dot(vals, w_two, NT)
            delta = jnp.sum(probs * dprobs, axis=0, keepdims=True)
            p_buf[:, pair * 256:(pair + 1) * 256] = probs.astype(BF16)
            dscores = (probs * (dprobs - delta)).astype(BF16)
            dq = dot(kt_buf[...], dscores, NN) * scale
            dq = dq.astype(BF16).astype(F32)
            first, second = dq[0:64], dq[64:128]
            out = jnp.concatenate(
                [first * cosine + second * sine, second * cosine - first * sine], axis=0
            ).astype(BF16)
            base = h * GROUP * HEAD + 2 * pair * HEAD
            dq_ref[pl.ds(pl.multiple_of(base, HEAD), HEAD), :] = out[:, 0:ROWS]
            dq_ref[pl.ds(pl.multiple_of(base + HEAD, HEAD), HEAD), :] = out[:, ROWS:]
        dv = dot(p_buf[...], w_buf[...], NN)
        dv_ref[:, pl.ds(pl.multiple_of(h * HEAD, HEAD), HEAD)] = dv.astype(BF16)
        return carry

    lax.fori_loop(0, KV, one_group, 0)

    for j in range(1, BLOCKS):
        @pl.when(c + j < 8)
        def _():
            doc_copy(j).wait_send()

    def drain(h, carry):
        @pl.when(y < 3)
        def _():
            hop_own(h).wait_send()

        @pl.when(core == 0)
        def _():
            pair_own(h).wait_send()

        @pl.when(y >= 1)
        def _():
            pair_near_up(h).wait_send()

            @pl.when(y < 3)
            def _():
                hop_relay(h).wait_send()

        @pl.when(jnp.logical_and(y >= 2, core == 1))
        def _():
            pair_far_down(h).wait_send()
        return carry

    lax.fori_loop(0, KV, drain, 0)


def attention(q, g, lw, docs, k, v):
    vmem = pl.BlockSpec(memory_space=pltpu.VMEM)
    return pl.pallas_call(
        attention_kernel,
        out_shape=(
            jax.ShapeDtypeStruct((QW, ROWS), BF16),
            jax.ShapeDtypeStruct((WINDOW, KV * HEAD), BF16),
        ),
        in_specs=[vmem] * 6 + [pl.BlockSpec(memory_space=pl.ANY)],
        out_specs=(vmem, vmem),
        scratch_shapes=[
            pltpu.VMEM((KV, BLOCKS, 2, ROWS, HEAD), BF16),
            pltpu.VMEM((BLOCKS, 8, ROWS), F32),
            pltpu.VMEM((WINDOW, 2 * ROWS), F32),
            pltpu.VMEM((ROWS, ROWS), F32),
            pltpu.VMEM((2, HEAD // 2, ROWS), F32),
            pltpu.VMEM((WINDOW, GROUP * ROWS), BF16),
            pltpu.VMEM((GROUP * ROWS, HEAD), BF16),
            pltpu.VMEM((HEAD, WINDOW), BF16),
            pltpu.SemaphoreType.DMA,
            pltpu.SemaphoreType.DMA((BLOCKS - 1,)),
            pltpu.SemaphoreType.DMA((BLOCKS - 1,)),
            pltpu.SemaphoreType.DMA((KV, 5)),
            pltpu.SemaphoreType.DMA((KV, BLOCKS - 1)),
        ],
        compiler_params=pltpu.CompilerParams(
            collective_id=0, has_side_effects=True, vmem_limit_bytes=48 * 1024 * 1024),
        cost_estimate=pl.CostEstimate(
            flops=8 * 64 * WINDOW * ROWS * HEAD, bytes_accessed=10_000_000,
            transcendentals=64 * WINDOW * ROWS),
        name="attention_back",
    )(q, g, lw, docs, k, v, jnp.asarray(rope_tables()))


def reduce_kernel(
    dq_ref, dv_ref, x_ref, f_ref, m1_ref, m2_ref,
    o1_ref, o2_ref, o3_ref,
    grad, low_buf, mid_part, mid_buf, core_buf, stage, ry, rx, s2a, s2b, ry2, rx2,
    total, z_out, rz, z_sum, full,
    low_send, low_recv, mid_send, mid_recv, core_send, core_recv,
    y_send, y_recv, x_send, x_recv, x2_send, x2_recv, y2_send, y2_recv,
    z_send, z_recv, f_send, f_recv,
):
    dp = lax.axis_index("dp")
    c = lax.axis_index("ctx")
    x, z = dp // NZ, dp % NZ
    y, core = c // 2, c % 2
    own = BLOCKS - 1

    def at(xx, zz, yy, cc):
        return (xx * NZ + zz, yy * 2 + cc)

    def ahead(value, step, size):
        return (value + step) % size

    def push(src, dst, send, recv, peer):
        return pltpu.make_async_remote_copy(
            src_ref=src, dst_ref=dst, send_sem=send, recv_sem=recv,
            device_id=peer, device_id_type=MESH)

    barrier = pltpu.get_barrier_semaphore()
    peers = [(dp, ahead(c, j, 8)) for j in range(1, 8)]
    peers += [at(ahead(x, d, NX), z, y, core) for d in range(1, NX)]
    peers += [at(x, ahead(z, d, NZ), y, core) for d in range(1, NZ)]
    for peer in peers:
        pl.semaphore_signal(barrier, inc=1, device_id=peer, device_id_type=MESH)

    low_q = dot(f_ref[:, 0:D], x_ref[...], NT).astype(BF16)
    low_v = dot(f_ref[:, D:2 * D], x_ref[...], NT).astype(BF16)
    low_buf[own] = low_v
    for slot in range(own):
        @pl.when(c + slot < own)
        def _():
            low_buf[slot] = jnp.zeros((RANK, ROWS), BF16)

        @pl.when(c + slot + 1 > 7)
        def _():
            mid_buf[slot] = jnp.zeros((RANK, ROWS), F32)

    part = dot(f_ref[:, BV:FACT], dv_ref[...], NT)
    for slot in range(BLOCKS):
        mid_part[slot] = part[:, slot * ROWS:(slot + 1) * ROWS]

    pl.semaphore_wait(barrier, len(peers))

    def low_copy(j):
        return push(low_buf.at[own], low_buf.at[own - j], low_send.at[j - 1],
                    low_recv.at[own - j], (dp, c + j))

    def mid_copy(j):
        return push(mid_part.at[own - j], mid_buf.at[j - 1], mid_send.at[j - 1],
                    mid_recv.at[j - 1], (dp, c - j))

    for j in range(1, BLOCKS):
        @pl.when(c + j < 8)
        def _():
            low_copy(j).start()

        @pl.when(c >= j)
        def _():
            mid_copy(j).start()

    mid_q = dot(f_ref[:, BQ:BV], dq_ref[...], NN).astype(BF16)
    for i in range(KV):
        grad[:, BQ + i * 1024:BQ + (i + 1) * 1024] = dot(
            low_q, dq_ref[i * 1024:(i + 1) * 1024, :], NT)
    for slot in range(own):
        @pl.when(c + slot >= own)
        def _():
            low_copy(own - slot).wait_recv()
    low_window = jnp.concatenate([low_buf[s] for s in range(BLOCKS)], axis=1)
    grad[:, BV:FACT] = dot(low_window, dv_ref[...], NN)

    def core_copy(part_x):
        return push(
            grad.at[:, pl.ds(pl.multiple_of(part_x * XCOLS + (1 - core) * HALF, HEAD), HALF)],
            core_buf.at[part_x], core_send.at[part_x], core_recv.at[part_x],
            at(x, z, y, 1 - core))

    core_copy(3).start()
    for i in range(5):
        cols = slice(i * 1024, (i + 1) * 1024)
        grad[:, cols] = dot(mid_q, x_ref[:, cols], NN)
    core_copy(0).start()
    mid_v = mid_part[own]
    for j in range(1, BLOCKS):
        @pl.when(c + j < 8)
        def _():
            mid_copy(j).wait_recv()
        mid_v = mid_v + mid_buf[j - 1]
    mid_v = mid_v.astype(BF16)
    for i in range(5):
        grad[:, D + i * 1024:D + (i + 1) * 1024] = dot(
            mid_v, x_ref[:, i * 1024:(i + 1) * 1024], NN)
    core_copy(1).start()
    core_copy(2).start()

    def y_rows(yy):
        return pl.ds(pl.multiple_of(yy * 16, 16), 16)

    def y_copy(d, part_x):
        yy = ahead(y, d, NY)
        return push(stage.at[part_x, y_rows(yy), 0:CUT], ry.at[d - 1, part_x],
                    y_send.at[d - 1, part_x], y_recv.at[d - 1, part_x], at(x, z, yy, core))

    def x_copy(d):
        xx = ahead(x, d, NX)
        return push(stage.at[xx, :, CUT:HALF], rx.at[d - 1],
                    x_send.at[d - 1], x_recv.at[d - 1], at(xx, z, y, core))

    for part_x in (3, 0, 1, 2):
        core_copy(part_x).wait_recv()
        mine = grad[:, pl.ds(pl.multiple_of(part_x * XCOLS + core * HALF, HEAD), HALF)]
        stage[part_x] = (mine + core_buf[part_x]).astype(BF16)
        for d in range(1, NY):
            y_copy(d, part_x).start()
        for d in range(1, NX):
            @pl.when(ahead(x, d, NX) == part_x)
            def _():
                x_copy(d).start()

    def x2_copy(d):
        return push(s2a.at[d - 1], rx2.at[d - 1], x2_send.at[d - 1], x2_recv.at[d - 1],
                    at(ahead(x, d, NX), z, y, core))

    def y2_copy(d):
        return push(s2b.at[d - 1], ry2.at[d - 1], y2_send.at[d - 1], y2_recv.at[d - 1],
                    at(x, z, ahead(y, d, NY), core))

    for part_x in (3, 0, 1, 2):
        for d in range(1, NY):
            y_copy(d, part_x).wait_recv()
    for d in (1, 2, 3, 0):
        xx = ahead(x, d, NX)
        value = stage[xx, y_rows(y), 0:CUT].astype(F32)
        for e in range(NY - 1):
            value = value + ry[e, xx].astype(F32)
        if d:
            s2a[d - 1] = value.astype(BF16)
            x2_copy(d).start()
        else:
            total[:, 0:CUT] = value
    for d in range(1, NX):
        x_copy(d).wait_recv()
    for d in (1, 2, 3, 0):
        yy = ahead(y, d, NY)
        value = stage[x, y_rows(yy), CUT:HALF].astype(F32)
        for e in range(NX - 1):
            value = value + rx[e, y_rows(yy), :].astype(F32)
        if d:
            s2b[d - 1] = value.astype(BF16)
            y2_copy(d).start()
        else:
            total[:, CUT:HALF] = value
    for d in range(1, NX):
        x2_copy(d).wait_recv()
    value = total[:, 0:CUT]
    for e in range(NX - 1):
        value = value + rx2[e].astype(F32)
    total[:, 0:CUT] = value
    for d in range(1, NY):
        y2_copy(d).wait_recv()
    value = total[:, CUT:HALF]
    for e in range(NY - 1):
        value = value + ry2[e].astype(F32)
    total[:, CUT:HALF] = value
    z_out[...] = total[...].astype(BF16)

    starts = (0, 512, 1152, 1664)

    def z_copy(quarter, slot):
        return push(z_out.at[:, starts[quarter]:starts[quarter] + WIN], rz.at[slot],
                    z_send.at[quarter], z_recv.at[slot], at(x, core * 4 + quarter, y, core))

    for quarter in range(4):
        @pl.when(core * 4 + quarter != z)
        def _():
            z_copy(quarter, z).start()

    def full_copy(j):
        return push(full.at[y_rows(y)], full.at[y_rows(y)], f_send.at[j - 1],
                    f_recv.at[y], (dp, ahead(c, j, 8)))

    holder = z // 4

    @pl.when(core == holder)
    def _():
        for quarter in range(4):
            @pl.when(z % 4 == quarter)
            def _():
                z_sum[...] = total[:, starts[quarter]:starts[quarter] + WIN]
        value = z_sum[...]
        for s in range(1, NZ):
            slot = ahead(z, s, NZ)
            z_copy(0, slot).wait_recv()
            value = value + rz[slot].astype(F32)
        for quarter in range(4):
            @pl.when(z % 4 == quarter)
            def _():
                shift = quarter * SHARD - starts[quarter]
                moved = pltpu.roll(value, WIN - shift, axis=1) if shift else value
                full[y_rows(y), :] = moved[:, 0:640]
        for j in range(1, 8):
            full_copy(j).start()

    def row_wait(yy):
        pltpu.make_async_remote_copy(
            src_ref=full.at[y_rows(yy)], dst_ref=full.at[y_rows(yy)], send_sem=f_send.at[0],
            recv_sem=f_recv.at[yy], device_id=(dp, ahead(c, 1, 8)),
            device_id_type=MESH).wait_recv()

    for d in range(1, NY):
        row_wait(ahead(y, d, NY))

    @pl.when(core != holder)
    def _():
        row_wait(y)

    gradient = full[:, 0:SHARD] * (ADAPTER_SCALE / (NX * NZ))
    new_m = BETA_ONE * m1_ref[...] + (1.0 - BETA_ONE) * gradient
    new_v = BETA_TWO * m2_ref[...] + (1.0 - BETA_TWO) * gradient * gradient
    corr_one = 1.0 - BETA_ONE ** STEP_COUNT
    corr_two = 1.0 - BETA_TWO ** STEP_COUNT
    o1_ref[...] = new_m
    o2_ref[...] = new_v
    o3_ref[...] = new_m / corr_one / (jnp.sqrt(new_v / corr_two) + ADAM_EPS)

    for j in range(1, BLOCKS):
        @pl.when(c + j < 8)
        def _():
            low_copy(j).wait_send()

        @pl.when(c >= j)
        def _():
            mid_copy(j).wait_send()
    for part_x in range(NX):
        core_copy(part_x).wait_send()
        for d in range(1, NY):
            y_copy(d, part_x).wait_send()
    for d in range(1, NX):
        x_copy(d).wait_send()
        x2_copy(d).wait_send()
        y2_copy(d).wait_send()
    for quarter in range(4):
        @pl.when(core * 4 + quarter != z)
        def _():
            z_copy(quarter, z).wait_send()

    @pl.when(core == holder)
    def _():
        for j in range(1, 8):
            full_copy(j).wait_send()


def reduce_and_step(dq, dv, x, factors, m1, m2):
    vmem = pl.BlockSpec(memory_space=pltpu.VMEM)
    dma = pltpu.SemaphoreType.DMA
    out = jax.ShapeDtypeStruct((RANK, SHARD), F32)
    return pl.pallas_call(
        reduce_kernel,
        out_shape=(out, out, out),
        in_specs=[vmem] * 6,
        out_specs=(vmem, vmem, vmem),
        scratch_shapes=[
            pltpu.VMEM((RANK, FACT), F32),
            pltpu.VMEM((BLOCKS, RANK, ROWS), BF16),
            pltpu.VMEM((BLOCKS, RANK, ROWS), F32),
            pltpu.VMEM((BLOCKS - 1, RANK, ROWS), F32),
            pltpu.VMEM((NX, RANK, HALF), F32),
            pltpu.VMEM((NX, RANK, HALF), BF16),
            pltpu.VMEM((NY - 1, NX, 16, CUT), BF16),
            pltpu.VMEM((NX - 1, RANK, REST), BF16),
            pltpu.VMEM((NX - 1, 16, CUT), BF16),
            pltpu.VMEM((NY - 1, 16, REST), BF16),
            pltpu.VMEM((NY - 1, 16, REST), BF16),
            pltpu.VMEM((NX - 1, 16, CUT), BF16),
            pltpu.VMEM((16, HALF), F32),
            pltpu.VMEM((16, HALF), BF16),
            pltpu.VMEM((NZ, 16, WIN), BF16),
            pltpu.VMEM((16, WIN), F32),
            pltpu.VMEM((RANK, 640), F32),
            dma((4,)), dma((4,)), dma((4,)), dma((4,)), dma((4,)), dma((4,)),
            dma((3, 4)), dma((3, 4)), dma((3,)), dma((3,)),
            dma((3,)), dma((3,)), dma((3,)), dma((3,)),
            dma((4,)), dma((8,)), dma((7,)), dma((4,)),
        ],
        compiler_params=pltpu.CompilerParams(
            collective_id=1, has_side_effects=True, vmem_limit_bytes=48 * 1024 * 1024),
        cost_estimate=pl.CostEstimate(
            flops=4 * FACT * RANK * ROWS, bytes_accessed=10_000_000, transcendentals=0),
        name="reduce_and_step",
    )(dq, dv, x, factors, m1, m2)


def per_device(
    normed_input, queries, keys, values, out_grad, loss_weight, doc_ids, adapter, moment1, moment2
):
    factors = lax.all_gather(adapter.astype(BF16), "dp", axis=1, tiled=True)
    dq, dv = attention(
        queries[0], out_grad[0], loss_weight, doc_ids, keys[0], values[0])
    return reduce_and_step(dq, dv, normed_input[0], factors, moment1, moment2)


def solution(mesh):
    in_specs = (
        P("dp", "ctx", None),
        P("dp", "ctx", None),
        P("dp", "ctx", None),
        P("dp", "ctx", None),
        P("dp", "ctx", None),
        P("dp", "ctx"),
        P("dp", "ctx"),
        P(None, "dp"),
        P(None, "dp"),
        P(None, "dp"),
    )
    out_specs = (P(None, "dp"), P(None, "dp"), P(None, "dp"))
    return jax.shard_map(
        per_device, mesh=mesh, in_specs=in_specs, out_specs=out_specs, check_vma=False
    )
```

time: 867 us -> 155 us (0.18); the launches traced: 855 us -> 154 us
  waiting for transfers between devices: 320 us -> 45 us
  other arithmetic: 153 us -> 1.56 us
  local copies, waits for them, and re-layouts: 170 us -> 21.7 us
  matrix products: 116 us -> 0 us
  Pallas kernels: 0 us -> 72 us
  starting transfers between devices: 42.3 us -> 0.04 us
  blocking collectives: 28.3 us -> 0 us
  loops' own time: 11.6 us -> 0 us
    unnamed x4 -> x1, waiting for transfers between devices: 230 us -> 0.02 us
    dot_general x68 -> x0, matrix products: 116 us -> none  [the longest x16 40.5 us: one_block(): lax.dot_general(probs_b, g_rows, (((0,), (0,)), ((), ())), preferred_elem...]
    unnamed x8 -> x1, other arithmetic: 114 us -> 1.56 us
    pallas_call x0 -> x2, Pallas kernels: none -> 72 us  [the longest x1 40.8 us: reduce_and_step(): pl.pallas_call(reduce_kernel, out_shape=(out, out, out), in_specs=[vmem]...]
    unnamed x46 -> x24, local copies, waits for them, and re-layouts: 84.2 us -> 16.9 us
    psum x1 -> x0, waiting for transfers between devices: 66.2 us -> none  [per_device(): shard = lax.psum(shard, 'ctx')]
    all_gather x1, waiting for transfers between devices: 0.02 us -> 45 us  [per_device(): factors = lax.all_gather(adapter.astype(BF16), 'dp', axis=1, tiled=True)]
    all_to_all x6 -> x0, starting transfers between devices: 42.3 us -> none  [the longest x1 16.9 us: per_device(): lax.all_to_all(weighted_values, 'ctx', split_axis=2, concat_axis=1, tiled...]
  transfers between devices with their start and end apart: 9 -> 1, of which waited for: 4 -> 1; matrix products, arithmetic and copies ran while one was open for 45% -> 0% of each run, Pallas kernels for 0% -> 20%
where the time goes in v1:
time: 155 us; the launch traced here: 154 us
  Pallas kernels  72 us (46%)
  waiting for transfers between devices  45 us (29%)
  local copies, waits for them, and re-layouts  21.7 us (14%)
  between operations  14.1 us (9%)
  other arithmetic  1.56 us (1%)
    all_gather x1, waiting for transfers between devices, per_device(): factors = lax.all_gather(adapter.astype(BF16), 'dp', axis=1, tiled=True)  45 us
    pallas_call x1, Pallas kernels, reduce_and_step(): pl.pallas_call(reduce_kernel, out_shape=(out, out, out), in_specs=[vmem]...  40.8 us
    pallas_call x1, Pallas kernels, attention(): pl.pallas_call(attention_kernel, out_shape=(jax.ShapeDtypeStruct((QW, ROW...  31.2 us
    unnamed x24, local copies, waits for them, and re-layouts  16.9 us
    all_gather x1, local copies, waits for them, and re-layouts, per_device(): factors = lax.all_gather(adapter.astype(BF16), 'dp', axis=1, tiled=True)  4.76 us
  transfers between devices with their start and end apart: 1, of which 1 were waited for; matrix products, arithmetic and copies ran while one was open for 0% of the time, Pallas kernels for 20%

profile of v1, /device:TPU:1, one launch (start us, length us, event | category | flops | bytes accessed | tf_op | source)
XLA Modules:
  0.0 154.3 jit_solution(7380172785703696482)
XLA Ops:
  7.2 0.0 all-gather.3.cloned.1.call-start
  7.2 1.6 %convert_bitcast_fusion = bf16[1,608,64]{1,2,0:T(8,128)(2,1)} fusion(f32[64,608]{1,0:T(8,128)} %param.18), kind=kLoop, calls=%fused_computation | loop fusion | flops 38912 | bytes 233472
  8.8 0.0 all-gather.3.cloned.1.call-update
  8.8 0.0 copy-start.5
  8.8 0.9 copy-done.5
  9.8 0.0 copy-start.6
  9.8 0.9 copy-done.6
  10.7 0.0 copy-start.7
  10.7 0.7 copy-done.7
  11.4 0.0 copy-start.8
  11.4 0.7 copy-done.8
  12.0 0.0 copy-start.9
  12.0 1.0 copy-done.9
  13.1 31.2 %attention_back.1 = (bf16[8192,128]{1,0:T(8,128)(2,1)S(1)}, bf16[640,1024]{1,0:T(8,128)(2,1)S(1)}) custom-call(bf16[128,8192]{1,0:T(8,128)(2,1)} %bitcast.16, bf16[128,8192]{1,0:T(8,128)(2,1)} %bitcast.17, s32[1,128]{1,0:T(1,128)S(1)} %copy-done.7, s32[1,128]{1,0:T(1,128)S(1)} %copy-done.8, bf16[128,1024]{1,0:T(8,128)(2,1)S(1)} %bitcast.13, ...), custom_call_target="tpu_custom_call" | custom-call | flops 5368709120 | bytes 10000000 | tf_op jit(solution)/shard_map/attention_back/pallas_call | solution.py:280
  44.3 0.0 copy-start.1
  44.3 1.1 copy-done.1
  45.4 45.0 %all-gather.3.cloned.1.call-done = bf16[32,608,64]{1,2,0:T(8,128)(2,1)} async-done(((bf16[1,608,64]{1,2,0:T(8,128)(2,1)}), bf16[32,608,64]{1,2,0:T(8,128)(2,1)}) %all-gather.3.cloned.1.call-update) | async-done | bytes 2490384 | tf_op jit(solution)/shard_map/all_gather | solution.py:615
  90.3 4.8 %copy.15 = bf16[32,608,64]{1,0,2:T(8,128)(2,1)} copy(bf16[32,608,64]{1,2,0:T(8,128)(2,1)} %all-gather.3.cloned.1.call-done) | data formatting | bytes 4980736 | tf_op jit(solution)/shard_map/all_gather | solution.py:615
  95.1 0.0 copy-start
  95.1 6.4 %reshape.7 = bf16[19456,64]{0,1:T(8,128)(2,1)} reshape(bf16[32,608,64]{1,0,2:T(8,128)(2,1)} %copy.15) | data formatting | bytes 4980736
  101.5 0.0 copy-done
  101.5 0.0 copy-start.2
  101.5 1.3 copy-done.2
  102.8 0.0 copy-start.3
  102.9 0.9 copy-done.3
  103.8 0.0 copy-start.4
  103.8 0.9 copy-done.4
  104.7 40.8 %reduce_and_step.1 = (f32[64,608]{1,0:T(8,128)S(1)}, f32[64,608]{1,0:T(8,128)S(1)}, f32[64,608]{1,0:T(8,128)S(1)}) custom-call(bf16[8192,128]{1,0:T(8,128)(2,1)S(1)} %get-tuple-element.5.dq_ref, bf16[640,1024]{1,0:T(8,128)(2,1)S(1)} %copy-done.2, bf16[128,5120]{1,0:T(8,128)(2,1)S(1)} %bitcast.12, bf16[64,19456]{1,0:T(8,128)(2,1)} %bitcast.15, ...), custom_call_target="tpu_custom_call" | custom-call | flops 637534208 | bytes 10000000 | tf_op jit(solution)/shard_map/reduce_and_step/pallas_call | solution.py:576
  145.5 0.7 copy.19
  146.1 0.7 copy.20
  146.8 0.7 copy.21
Async XLA Ops:
  7.2 83.2 %all-gather.3.cloned.1.call-start = ((), (), s32[]{:S(2)}) async-start(), calls=%async_computation | async-start | bytes 2703360 | tf_op jit(solution)/shard_map/all_gather | solution.py:615
  8.8 1.0 copy-start.5
  9.8 0.9 copy-start.6
  10.7 0.7 copy-start.7
  11.4 0.7 copy-start.8
  12.0 1.0 copy-start.9
  44.3 1.1 copy-start.1
  95.1 6.4 %copy-start = (bf16[1,128,5120]{2,1,0:T(8,128)(2,1)S(1)}, bf16[1,128,5120]{2,1,0:T(8,128)(2,1)}, u32[]{:S(2)}) copy-start(bf16[1,128,5120]{2,1,0:T(8,128)(2,1)} %param.11) | copy-start | bytes 3932164
  101.5 1.3 copy-start.2
  102.8 0.9 copy-start.3
  103.8 0.9 copy-start.4
Sparse Core Ops, SparseCore 0:
  11.2 79.1 all-gather.2

commit v2 on v1

v2 whole, which is shorter than its diff:
```python
import functools

import jax
import jax.numpy as jnp
import numpy as np
from jax import lax
from jax.experimental import pallas as pl
from jax.experimental.pallas import tpu as pltpu
from jax.sharding import PartitionSpec as P

HEAD = 128
GROUP = 8
KV = 8
D = 5120
RANK = 64
ROWS = 128
BLOCKS = 5
WINDOW = BLOCKS * ROWS
QW = KV * GROUP * HEAD
FACT = 2 * D + QW + KV * HEAD
BQ = 2 * D
BV = BQ + QW
NX, NZ, NY, NC = 4, 8, 4, 2
SHARD = FACT // (NX * NZ)
XCOLS = FACT // NX
HALF = XCOLS // 2
HALF_ROWS = RANK // 2
CUT = 1152
REST = HALF - CUT
WIN = 768

THETA = 1000000.0
ADAPTER_SCALE = 2.0
BETA_ONE = 0.9
BETA_TWO = 0.95
ADAM_EPS = 1e-08
STEP_COUNT = 10
NEG = -1e30
MESH = pl.DeviceIdType.MESH
NT = (((1,), (1,)), ((), ()))
NN = (((1,), (0,)), ((), ()))
F32 = jnp.float32
BF16 = jnp.bfloat16


def rope_tables():
    freq = THETA ** (-(np.arange(HEAD // 2, dtype=np.float64) * 2.0 / HEAD))
    angle = np.arange(NY * NC * ROWS, dtype=np.float64)[:, None] * freq[None, :]
    cosine, sine = np.cos(angle), np.sin(angle)
    both = np.stack(
        [np.concatenate([cosine, cosine], axis=1), np.concatenate([sine, -sine], axis=1)])
    return both.reshape(2, NY * NC, ROWS, HEAD).transpose(1, 0, 2, 3).astype(np.float32)


def dot(a, b, dims):
    return lax.dot_general(a, b, dims, preferred_element_type=F32)


def turn(a):
    return a.astype(F32).T.astype(BF16)


def kernel(
    q_hbm, g_hbm, lw_hbm, docs_hbm, k_hbm, v_hbm, x_hbm, a_hbm, table_hbm,
    out_ref,
    q_ref, g_ref, lw_ref, docs_ref, x_ref, a_ref, table,
    kv_buf, back_buf, doc_buf, bias, lw_t, w_buf, dq_ref, dv_ref,
    a_roll, z_in, f_ref,
    grad, low_buf, mid_part, mid_buf, core_buf, stage, ry, rx, s2a, s2b, ry2, rx2,
    total, z_out, rz, z_sum, full,
    in_sem, q_sem, g_sem, kv_sem, doc_send, doc_recv, send_sem, recv_sem, back_recv,
    fz_send, fz_recv, fx_send, fx_recv, fc_send, fc_recv,
    low_send, low_recv, mid_send, mid_recv, core_send, core_recv,
    y_send, y_recv, x_send, x_recv, x2_send, x2_recv, y2_send, y2_recv,
    z_send, z_recv, f_send, f_recv,
):
    dp = lax.axis_index("dp")
    c = lax.axis_index("ctx")
    x, z = dp // NZ, dp % NZ
    y, core = c // 2, c % 2
    own = BLOCKS - 1

    def at(xx, zz, yy, cc):
        return (xx * NZ + zz, yy * 2 + cc)

    def ahead(value, step, size):
        return (value + step) % size

    def push(src, dst, send, recv, peer):
        return pltpu.make_async_remote_copy(
            src_ref=src, dst_ref=dst, send_sem=send, recv_sem=recv,
            device_id=peer, device_id_type=MESH)

    def cols_of(h, width):
        return pl.ds(pl.multiple_of(h * width, width), width)

    def kv_load(h, which):
        source = k_hbm if which == 0 else v_hbm
        return pltpu.make_async_copy(
            source.at[:, cols_of(h, HEAD)], kv_buf.at[h, own, which], kv_sem.at[h, which])

    def q_load(h):
        return pltpu.make_async_copy(
            q_hbm.at[:, cols_of(h, 1024)], q_ref.at[:, cols_of(h, 1024)], q_sem.at[h])

    def g_load(h):
        return pltpu.make_async_copy(
            g_hbm.at[:, cols_of(h, 1024)], g_ref.at[:, cols_of(h, 1024)], g_sem.at[h])

    small = [
        pltpu.make_async_copy(docs_hbm, docs_ref, in_sem.at[0]),
        pltpu.make_async_copy(a_hbm, a_ref, in_sem.at[1]),
        pltpu.make_async_copy(lw_hbm, lw_ref, in_sem.at[2]),
        pltpu.make_async_copy(table_hbm.at[c], table, in_sem.at[3]),
        pltpu.make_async_copy(x_hbm, x_ref, in_sem.at[4]),
    ]
    barrier = pltpu.get_barrier_semaphore()
    peers = [(dp, ahead(c, j, 8)) for j in range(1, 8)]
    peers += [at(ahead(x, d, NX), z, y, core) for d in range(1, NX)]
    peers += [at(x, ahead(z, d, NZ), y, core) for d in range(1, NZ)]
    for peer in peers:
        pl.semaphore_signal(barrier, inc=1, device_id=peer, device_id_type=MESH)
    small[0].start()
    small[1].start()

    def load_kv(h, carry):
        kv_load(h, 0).start()
        kv_load(h, 1).start()
        return carry

    lax.fori_loop(0, KV, load_kv, 0)
    small[2].start()
    small[3].start()

    def load_qg(h, carry):
        q_load(h).start()
        g_load(h).start()
        return carry

    lax.fori_loop(0, KV, load_qg, 0)
    small[4].start()

    for slot in range(own):
        @pl.when(c + slot < own)
        def _():
            doc_buf[slot] = jnp.full((8, ROWS), -1.0, F32)
            low_buf[slot] = jnp.zeros((RANK, ROWS), BF16)
            for h in range(KV):
                kv_buf[h, slot] = jnp.zeros((2, ROWS, HEAD), BF16)

        @pl.when(c + slot + 1 > 7)
        def _():
            mid_buf[slot] = jnp.zeros((RANK, ROWS), F32)

    small[0].wait()
    doc_buf[own] = jnp.broadcast_to(docs_ref[...].astype(F32), (8, ROWS))
    pl.semaphore_wait(barrier, len(peers))

    def doc_copy(j):
        return push(doc_buf.at[own], doc_buf.at[own - j], doc_send.at[j - 1],
                    doc_recv.at[own - j], (dp, c + j))

    def kv_copy(h, kind, source, target, peer):
        return push(kv_buf.at[h, source], kv_buf.at[h, target], send_sem.at[h, kind],
                    recv_sem.at[h, target], (dp, peer))

    def hop_own(h):
        return kv_copy(h, 0, 4, 2, c + 2)

    def pair_own(h):
        return kv_copy(h, 1, 4, 3, c + 1)

    def hop_relay(h):
        return kv_copy(h, 2, 2, 0, c + 2)

    def pair_near_up(h):
        return kv_copy(h, 3, 2, 1, c + 1)

    def pair_near_down(h):
        return kv_copy(h, 3, 2, 3, c - 1)

    def pair_far_down(h):
        return kv_copy(h, 4, 0, 1, c - 1)

    def back_own(h):
        return push(kv_buf.at[h, own], back_buf.at[h], send_sem.at[h, 5], back_recv.at[h],
                    (dp, ahead(c, 6, 8)))

    def back_relay(h):
        return push(back_buf.at[h], kv_buf.at[h, 0], send_sem.at[h, 6], recv_sem.at[h, 0],
                    (dp, ahead(c, 6, 8)))

    def is_back(h):
        return h % 2 == 1

    outer = jnp.logical_or(y == 0, y == 3)

    def send_own(h, carry):
        kv_load(h, 0).wait()
        kv_load(h, 1).wait()

        @pl.when(y < 3)
        def _():
            hop_own(h).start()

        @pl.when(core == 0)
        def _():
            pair_own(h).start()

        @pl.when(jnp.logical_and(is_back(h), y < 2))
        def _():
            back_own(h).start()
        return carry

    send_own(0, 0)
    for j in range(1, BLOCKS):
        @pl.when(c + j < 8)
        def _():
            doc_copy(j).start()
    lax.fori_loop(1, KV, send_own, 0)

    rank_rows = pl.ds(pl.multiple_of(core * HALF_ROWS, HALF_ROWS), HALF_ROWS)
    block_cols = pl.ds(pl.multiple_of(x * XCOLS, HEAD), XCOLS)
    small[1].wait()
    a_roll[:, 512:WIN] = jnp.zeros((RANK, WIN - 512), F32)
    a_roll[:, 0:SHARD] = a_ref[...]
    offsets = (0, 96, 64, 32)
    for quarter in range(1, 4):
        @pl.when(z % 4 == quarter)
        def _():
            a_roll[...] = pltpu.roll(a_roll[...], offsets[quarter], axis=1)
    z_in[z] = a_roll[rank_rows, :].astype(BF16)

    def fz_copy(d):
        return push(z_in.at[z], z_in.at[z], fz_send.at[d - 1], fz_recv.at[d - 1],
                    at(x, ahead(z, d, NZ), y, core))

    def fz_wait(d):
        src = ahead(z, NZ - d, NZ)
        push(z_in.at[src], z_in.at[src], fz_send.at[d - 1], fz_recv.at[d - 1],
             at(x, ahead(z, d, NZ), y, core)).wait_recv()

    for d in range(1, NZ):
        fz_copy(d).start()

    def fx_copy(d):
        return push(f_ref.at[rank_rows, block_cols], f_ref.at[rank_rows, block_cols],
                    fx_send.at[d - 1], fx_recv.at[d - 1], at(ahead(x, d, NX), z, y, core))

    def section(xx):
        return pl.ds(pl.multiple_of(xx * XCOLS, HEAD), XCOLS)

    def fx_wait(d):
        src = ahead(x, NX - d, NX)
        push(f_ref.at[rank_rows, section(src)], f_ref.at[rank_rows, section(src)],
             fx_send.at[d - 1], fx_recv.at[d - 1], at(ahead(x, d, NX), z, y, core)).wait_recv()

    other_rows = pl.ds(pl.multiple_of((1 - core) * HALF_ROWS, HALF_ROWS), HALF_ROWS)

    def fc_copy(d):
        src = ahead(x, NX - d, NX)
        return push(f_ref.at[rank_rows, section(src)], f_ref.at[rank_rows, section(src)],
                    fc_send.at[d], fc_recv.at[d], at(x, z, y, 1 - core))

    def fc_wait(d):
        src = ahead(x, NX - d, NX)
        push(f_ref.at[other_rows, section(src)], f_ref.at[other_rows, section(src)],
             fc_send.at[d], fc_recv.at[d], at(x, z, y, 1 - core)).wait_recv()

    def gather_block():
        for d in range(1, NZ):
            fz_wait(d)
        for quad in range(2):
            w = [z_in[quad * 4 + i] for i in range(4)]
            pieces = [
                w[0][:, 0:512], w[0][:, 512:640] + w[1][:, 0:128],
                w[1][:, 128:640], w[1][:, 640:768] + w[2][:, 0:128],
                w[2][:, 128:640], w[2][:, 640:768] + w[3][:, 0:128],
                w[3][:, 128:640],
            ]
            where = pl.ds(pl.multiple_of(x * XCOLS + quad * HALF, HEAD), HALF)
            f_ref[rank_rows, where] = jnp.concatenate(pieces, axis=1)
        for d in range(1, NX):
            fx_copy(d).start()
        fc_copy(0).start()

    def relay_near(h):
        @pl.when(y >= 1)
        def _():
            hop_own(h).wait_recv()

            @pl.when(jnp.logical_and(jnp.logical_not(is_back(h)), y < 3))
            def _():
                hop_relay(h).start()

            @pl.when(core == 0)
            def _():
                pair_near_up(h).start()

            @pl.when(core == 1)
            def _():
                pair_near_down(h).start()

        @pl.when(jnp.logical_and(is_back(h), outer))
        def _():
            back_own(h).wait_recv()
            back_relay(h).start()

    def relay_far(h):
        @pl.when(y >= 2)
        def _():
            hop_relay(h).wait_recv()

            @pl.when(core == 1)
            def _():
                pair_far_down(h).start()

    def arrive(h):
        @pl.when(jnp.logical_or(core == 1, y >= 1))
        def _():
            pair_own(h).wait_recv()

        @pl.when(jnp.logical_or(y >= 2, jnp.logical_and(core == 1, y >= 1)))
        def _():
            pair_far_down(h).wait_recv()

    relay_near(0)
    relay_near(1)
    small[2].wait()
    lw_t[...] = jnp.broadcast_to(lw_ref[...].astype(F32), (ROWS, ROWS)).T
    for slot in range(own):
        @pl.when(c + slot >= own)
        def _():
            doc_copy(own - slot).wait_recv()
    doc_col = jnp.broadcast_to(doc_buf[own][0:1, :], (ROWS, ROWS)).T
    row_pos = lax.broadcasted_iota(jnp.int32, (ROWS, ROWS), 0)
    key_pos = lax.broadcasted_iota(jnp.int32, (ROWS, ROWS), 1)
    for slot in range(BLOCKS):
        allowed = jnp.broadcast_to(doc_buf[slot][0:1, :], (ROWS, ROWS)) == doc_col
        if slot == own:
            allowed = jnp.logical_and(allowed, key_pos <= row_pos)
        bias[:, slot * ROWS:(slot + 1) * ROWS] = jnp.where(allowed, 0.0, NEG)
    small[3].wait()
    relay_far(0)

    scale = 1.0 / HEAD ** 0.5
    fold = scale * float(np.log2(np.e))
    part_heads = 4

    def one_group(h, carry):
        @pl.when(h + 2 < KV)
        def _():
            relay_near(h + 2)

        @pl.when(h + 1 < KV)
        def _():
            relay_far(h + 1)

        @pl.when(h == 2)
        def _():
            gather_block()

        q_load(h).wait()
        g_load(h).wait()
        arrive(h)
        keys = kv_buf[h, :, 0].reshape(WINDOW, HEAD)
        vals = kv_buf[h, :, 1].reshape(WINDOW, HEAD)

        def head_cols(i):
            return pl.ds(pl.multiple_of(h * GROUP * HEAD + i * HEAD, HEAD), HEAD)

        def front(part):
            heads = range(part * part_heads, (part + 1) * part_heads)
            queries = jnp.concatenate([q_ref[:, head_cols(i)] for i in heads], axis=0)
            weighted = jnp.concatenate(
                [(g_ref[:, head_cols(i)].astype(F32) * lw_t[...]).astype(BF16) for i in heads],
                axis=0)
            w_buf[part] = weighted
            return dot(queries, keys, NT), dot(weighted, vals, NT)

        parts = GROUP // part_heads
        ready = front(0)
        dv = None
        for part in range(parts):
            scores, dprobs = ready
            if part + 1 < parts:
                ready = front(part + 1)
            probs_b, dscores = [], []
            for t in range(part_heads):
                rows = slice(t * ROWS, (t + 1) * ROWS)
                masked = scores[rows] + bias[...]
                top = jnp.max(masked, axis=1, keepdims=True)
                expo = jnp.exp2((masked - top) * fold)
                probs = expo * (1.0 / jnp.sum(expo, axis=1, keepdims=True))
                dp_rows = dprobs[rows]
                delta = jnp.sum(probs * dp_rows, axis=1, keepdims=True)
                probs_b.append(probs.astype(BF16))
                dscores.append((probs * (dp_rows - delta)).astype(BF16))
            dq = dot(jnp.concatenate(dscores, axis=0), keys, NN) * scale
            for t in range(part_heads):
                rot = dq[t * ROWS:(t + 1) * ROWS].astype(BF16).astype(F32)
                dq_ref[:, head_cols(part * part_heads + t)] = (
                    rot * table[0] + pltpu.roll(rot, HEAD // 2, axis=1) * table[1]).astype(BF16)
            more = dot(turn(w_buf[part]), jnp.concatenate(probs_b, axis=0), NN)
            dv = more if dv is None else dv + more
        dv_ref[cols_of(h, HEAD), :] = dv.astype(BF16)
        return carry

    lax.fori_loop(0, KV, one_group, 0)

    for d in range(1, NX):
        fx_wait(d)
        fc_copy(d).start()
    small[4].wait()
    for d in range(NX):
        fc_wait(d)

    def low_copy(j):
        return push(low_buf.at[own], low_buf.at[own - j], low_send.at[j - 1],
                    low_recv.at[own - j], (dp, c + j))

    def mid_copy(j):
        return push(mid_part.at[own - j], mid_buf.at[j - 1], mid_send.at[j - 1],
                    mid_recv.at[j - 1], (dp, c - j))

    low_buf[own] = dot(f_ref[:, D:2 * D], x_ref[...], NT).astype(BF16)
    for j in range(1, BLOCKS):
        @pl.when(c + j < 8)
        def _():
            low_copy(j).start()
    piece = dot(f_ref[:, BV:FACT], dv_ref[...], NN)
    for slot in range(BLOCKS):
        mid_part[slot] = piece[:, slot * ROWS:(slot + 1) * ROWS]
    for j in range(1, BLOCKS):
        @pl.when(c >= j)
        def _():
            mid_copy(j).start()

    low_q = dot(f_ref[:, 0:D], x_ref[...], NT).astype(BF16)
    for i in range(KV):
        grad[:, BQ + i * 1024:BQ + (i + 1) * 1024] = dot(
            low_q, dq_ref[:, i * 1024:(i + 1) * 1024], NN)
    for slot in range(own):
        @pl.when(c + slot >= own)
        def _():
            low_copy(own - slot).wait_recv()
    low_window = jnp.concatenate([low_buf[s] for s in range(BLOCKS)], axis=1)
    grad[:, BV:FACT] = dot(low_window, dv_ref[...], NT)

    def core_copy(part_x):
        return push(
            grad.at[:, pl.ds(pl.multiple_of(part_x * XCOLS + (1 - core) * HALF, HEAD), HALF)],
            core_buf.at[part_x], core_send.at[part_x], core_recv.at[part_x],
            at(x, z, y, 1 - core))

    core_copy(3).start()
    mid_q = dot(f_ref[:, BQ:BV], dq_ref[...], NT).astype(BF16)
    for i in range(5):
        cols = slice(i * 1024, (i + 1) * 1024)
        grad[:, cols] = dot(mid_q, x_ref[:, cols], NN)
    core_copy(0).start()
    mid_v = mid_part[own]
    for j in range(1, BLOCKS):
        @pl.when(c + j < 8)
        def _():
            mid_copy(j).wait_recv()
        mid_v = mid_v + mid_buf[j - 1]
    mid_v = mid_v.astype(BF16)
    for i in range(5):
        grad[:, D + i * 1024:D + (i + 1) * 1024] = dot(
            mid_v, x_ref[:, i * 1024:(i + 1) * 1024], NN)
    core_copy(1).start()
    core_copy(2).start()

    def y_rows(yy):
        return pl.ds(pl.multiple_of(yy * 16, 16), 16)

    def y_copy(d, part_x):
        yy = ahead(y, d, NY)
        return push(stage.at[part_x, y_rows(yy), 0:CUT], ry.at[d - 1, part_x],
                    y_send.at[d - 1, part_x], y_recv.at[d - 1, part_x], at(x, z, yy, core))

    def x_copy(d):
        xx = ahead(x, d, NX)
        return push(stage.at[xx, :, CUT:HALF], rx.at[d - 1],
                    x_send.at[d - 1], x_recv.at[d - 1], at(xx, z, y, core))

    for part_x in (3, 0, 1, 2):
        core_copy(part_x).wait_recv()
        mine = grad[:, pl.ds(pl.multiple_of(part_x * XCOLS + core * HALF, HEAD), HALF)]
        stage[part_x] = (mine + core_buf[part_x]).astype(BF16)
        for d in range(1, NY):
            y_copy(d, part_x).start()
        for d in range(1, NX):
            @pl.when(ahead(x, d, NX) == part_x)
            def _():
                x_copy(d).start()

    def x2_copy(d):
        return push(s2a.at[d - 1], rx2.at[d - 1], x2_send.at[d - 1], x2_recv.at[d - 1],
                    at(ahead(x, d, NX), z, y, core))

    def y2_copy(d):
        return push(s2b.at[d - 1], ry2.at[d - 1], y2_send.at[d - 1], y2_recv.at[d - 1],
                    at(x, z, ahead(y, d, NY), core))

    for part_x in (3, 0, 1, 2):
        for d in range(1, NY):
            y_copy(d, part_x).wait_recv()
    for d in (1, 2, 3, 0):
        xx = ahead(x, d, NX)
        value = stage[xx, y_rows(y), 0:CUT].astype(F32)
        for e in range(NY - 1):
            value = value + ry[e, xx].astype(F32)
        if d:
            s2a[d - 1] = value.astype(BF16)
            x2_copy(d).start()
        else:
            total[:, 0:CUT] = value
    for d in range(1, NX):
        x_copy(d).wait_recv()
    for d in (1, 2, 3, 0):
        yy = ahead(y, d, NY)
        value = stage[x, y_rows(yy), CUT:HALF].astype(F32)
        for e in range(NX - 1):
            value = value + rx[e, y_rows(yy), :].astype(F32)
        if d:
            s2b[d - 1] = value.astype(BF16)
            y2_copy(d).start()
        else:
            total[:, CUT:HALF] = value
    for d in range(1, NX):
        x2_copy(d).wait_recv()
    value = total[:, 0:CUT]
    for e in range(NX - 1):
        value = value + rx2[e].astype(F32)
    total[:, 0:CUT] = value
    for d in range(1, NY):
        y2_copy(d).wait_recv()
    value = total[:, CUT:HALF]
    for e in range(NY - 1):
        value = value + ry2[e].astype(F32)
    total[:, CUT:HALF] = value
    z_out[...] = total[...].astype(BF16)

    starts = (0, 512, 1152, 1664)

    def z_copy(quarter, slot):
        return push(z_out.at[:, starts[quarter]:starts[quarter] + WIN], rz.at[slot],
                    z_send.at[quarter], z_recv.at[slot], at(x, core * 4 + quarter, y, core))

    for quarter in range(4):
        @pl.when(core * 4 + quarter != z)
        def _():
            z_copy(quarter, z).start()

    def full_copy(j):
        return push(full.at[y_rows(y)], full.at[y_rows(y)], f_send.at[j - 1],
                    f_recv.at[y], (dp, ahead(c, j, 8)))

    holder = z // 4

    @pl.when(core == holder)
    def _():
        for quarter in range(4):
            @pl.when(z % 4 == quarter)
            def _():
                z_sum[...] = total[:, starts[quarter]:starts[quarter] + WIN]
        value = z_sum[...]
        for s in range(1, NZ):
            slot = ahead(z, s, NZ)
            z_copy(0, slot).wait_recv()
            value = value + rz[slot].astype(F32)
        for quarter in range(4):
            @pl.when(z % 4 == quarter)
            def _():
                shift = quarter * SHARD - starts[quarter]
                moved = pltpu.roll(value, WIN - shift, axis=1) if shift else value
                full[y_rows(y), :] = moved[:, 0:640]
        for j in range(1, 8):
            full_copy(j).start()

    def row_wait(yy):
        pltpu.make_async_remote_copy(
            src_ref=full.at[y_rows(yy)], dst_ref=full.at[y_rows(yy)], send_sem=f_send.at[0],
            recv_sem=f_recv.at[yy], device_id=(dp, ahead(c, 1, 8)),
            device_id_type=MESH).wait_recv()

    for d in range(1, NY):
        row_wait(ahead(y, d, NY))

    @pl.when(core != holder)
    def _():
        row_wait(y)

    out_ref[...] = full[...] * (ADAPTER_SCALE / (NX * NZ))

    for j in range(1, BLOCKS):
        @pl.when(c + j < 8)
        def _():
            doc_copy(j).wait_send()
            low_copy(j).wait_send()

        @pl.when(c >= j)
        def _():
            mid_copy(j).wait_send()

    def drain(h, carry):
        @pl.when(y < 3)
        def _():
            hop_own(h).wait_send()

        @pl.when(core == 0)
        def _():
            pair_own(h).wait_send()

        @pl.when(jnp.logical_and(is_back(h), y < 2))
        def _():
            back_own(h).wait_send()

        @pl.when(jnp.logical_and(is_back(h), outer))
        def _():
            back_relay(h).wait_send()

        @pl.when(y >= 1)
        def _():
            pair_near_up(h).wait_send()

        @pl.when(jnp.logical_and(jnp.logical_not(is_back(h)), jnp.logical_and(y >= 1, y < 3)))
        def _():
            hop_relay(h).wait_send()

        @pl.when(jnp.logical_and(y >= 2, core == 1))
        def _():
            pair_far_down(h).wait_send()
        return carry

    lax.fori_loop(0, KV, drain, 0)
    for d in range(1, NZ):
        fz_copy(d).wait_send()
    for d in range(1, NX):
        fx_copy(d).wait_send()
    for d in range(NX):
        fc_copy(d).wait_send()
    for part_x in range(NX):
        core_copy(part_x).wait_send()
        for d in range(1, NY):
            y_copy(d, part_x).wait_send()
    for d in range(1, NX):
        x_copy(d).wait_send()
        x2_copy(d).wait_send()
        y2_copy(d).wait_send()
    for quarter in range(4):
        @pl.when(core * 4 + quarter != z)
        def _():
            z_copy(quarter, z).wait_send()

    @pl.when(core == holder)
    def _():
        for j in range(1, 8):
            full_copy(j).wait_send()


def reduced_gradient(q, g, lw, docs, k, v, x, adapter):
    hbm = pl.BlockSpec(memory_space=pltpu.HBM)
    dma = pltpu.SemaphoreType.DMA
    mem = pltpu.VMEM
    return pl.pallas_call(
        kernel,
        out_shape=jax.ShapeDtypeStruct((RANK, 640), F32),
        in_specs=[hbm] * 9,
        out_specs=pl.BlockSpec(memory_space=pltpu.VMEM),
        scratch_shapes=[
            mem((ROWS, QW), BF16), mem((ROWS, QW), BF16),
            mem((1, ROWS), jnp.int32), mem((1, ROWS), jnp.int32),
            mem((ROWS, D), BF16), mem((RANK, SHARD), F32), mem((2, ROWS, HEAD), F32),
            mem((KV, BLOCKS, 2, ROWS, HEAD), BF16), mem((KV, 2, ROWS, HEAD), BF16),
            mem((BLOCKS, 8, ROWS), F32), mem((ROWS, WINDOW), F32), mem((ROWS, ROWS), F32),
            mem((2, 4 * ROWS, HEAD), BF16),
            mem((ROWS, QW), BF16), mem((KV * HEAD, WINDOW), BF16),
            mem((RANK, WIN), F32), mem((NZ, HALF_ROWS, WIN), BF16), mem((RANK, FACT), BF16),
            mem((RANK, FACT), F32), mem((BLOCKS, RANK, ROWS), BF16),
            mem((BLOCKS, RANK, ROWS), F32), mem((BLOCKS - 1, RANK, ROWS), F32),
            mem((NX, RANK, HALF), F32), mem((NX, RANK, HALF), BF16),
            mem((NY - 1, NX, 16, CUT), BF16), mem((NX - 1, RANK, REST), BF16),
            mem((NX - 1, 16, CUT), BF16), mem((NY - 1, 16, REST), BF16),
            mem((NY - 1, 16, REST), BF16), mem((NX - 1, 16, CUT), BF16),
            mem((16, HALF), F32), mem((16, HALF), BF16), mem((NZ, 16, WIN), BF16),
            mem((16, WIN), F32), mem((RANK, 640), F32),
            dma((5,)), dma((KV,)), dma((KV,)), dma((KV, 2)), dma((4,)), dma((4,)),
            dma((KV, 7)), dma((KV, 4)), dma((KV,)),
            dma((7,)), dma((7,)), dma((3,)), dma((3,)), dma((4,)), dma((4,)),
            dma((4,)), dma((4,)), dma((4,)), dma((4,)), dma((4,)), dma((4,)),
            dma((3, 4)), dma((3, 4)), dma((3,)), dma((3,)),
            dma((3,)), dma((3,)), dma((3,)), dma((3,)),
            dma((4,)), dma((8,)), dma((7,)), dma((4,)),
        ],
        compiler_params=pltpu.CompilerParams(
            collective_id=0, has_side_effects=True, vmem_limit_bytes=60 * 1024 * 1024),
        cost_estimate=pl.CostEstimate(
            flops=8 * 64 * WINDOW * ROWS * HEAD + 4 * FACT * RANK * ROWS,
            bytes_accessed=10_000_000, transcendentals=64 * WINDOW * ROWS),
        name="layer_back",
    )(q, g, lw, docs, k, v, x, adapter, jnp.asarray(rope_tables()))


def per_device(
    normed_input, queries, keys, values, out_grad, loss_weight, doc_ids, adapter, moment1, moment2
):
    gradient = reduced_gradient(
        queries[0], out_grad[0], loss_weight, doc_ids, keys[0], values[0], normed_input[0],
        adapter)[:, 0:SHARD]
    new_m = BETA_ONE * moment1 + (1.0 - BETA_ONE) * gradient
    new_v = BETA_TWO * moment2 + (1.0 - BETA_TWO) * gradient * gradient
    corr_one = 1.0 - BETA_ONE ** STEP_COUNT
    corr_two = 1.0 - BETA_TWO ** STEP_COUNT
    return (new_m, new_v, new_m / corr_one / (jnp.sqrt(new_v / corr_two) + ADAM_EPS))


def solution(mesh):
    in_specs = (
        P("dp", "ctx", None),
        P("dp", "ctx", None),
        P("dp", "ctx", None),
        P("dp", "ctx", None),
        P("dp", "ctx", None),
        P("dp", "ctx"),
        P("dp", "ctx"),
        P(None, "dp"),
        P(None, "dp"),
        P(None, "dp"),
    )
    out_specs = (P(None, "dp"), P(None, "dp"), P(None, "dp"))
    return jax.shard_map(
        per_device, mesh=mesh, in_specs=in_specs, out_specs=out_specs, check_vma=False
    )
```

time: 155 us -> 85.2 us (0.55)
  waiting for transfers between devices: 45 us -> 0 us
  local copies, waits for them, and re-layouts: 21.7 us -> 0.01 us
  between operations: 14.1 us -> 0.67 us
  Pallas kernels: 72 us -> 82.6 us
    all_gather x1 -> x0, waiting for transfers between devices: 45 us -> none  [per_device(): factors = lax.all_gather(adapter.astype(BF16), 'dp', axis=1, tiled=True)]
    unnamed x24 -> x4, local copies, waits for them, and re-layouts: 16.9 us -> 0.01 us
    pallas_call x2 -> x1, Pallas kernels: 72 us -> 82.6 us  [reduced_gradient(): pl.pallas_call(kernel, out_shape=jax.ShapeDtypeStruct((RANK, 640), F32),...]
    all_gather x1 -> x0, local copies, waits for them, and re-layouts: 4.76 us -> none  [per_device(): factors = lax.all_gather(adapter.astype(BF16), 'dp', axis=1, tiled=True)]
    div x0 -> x1, other arithmetic: none -> 1.74 us  [per_device(): new_m / corr_one / (jnp.sqrt(new_v / corr_two) + ADAM_EPS)]
    unnamed x1 -> x0, other arithmetic: 1.56 us -> none
  transfers between devices with their start and end apart: 1 -> 0, of which waited for: 1 -> 0; matrix products, arithmetic and copies ran while one was open for 0% -> 0% of each run, Pallas kernels for 20% -> 0%
where the time goes in v2:
time: 85.2 us; the launch traced here: 85.1 us
  Pallas kernels  82.6 us (97%)
  other arithmetic  1.74 us (2%)
    pallas_call x1, Pallas kernels, reduced_gradient(): pl.pallas_call(kernel, out_shape=jax.ShapeDtypeStruct((RANK, 640), F32),...  82.6 us
    div x1, other arithmetic, per_device(): new_m / corr_one / (jnp.sqrt(new_v / corr_two) + ADAM_EPS)  1.74 us

profile of v2, /device:TPU:1, one launch (start us, length us, event | category | flops | bytes accessed | tf_op | source)
XLA Modules:
  0.0 85.1 jit_solution(15349148733349655090)
XLA Ops:
  0.6 0.0 copy-start
  0.6 0.0 copy-start.1
  0.7 82.6 %layer_back.1 = f32[64,640]{1,0:T(8,128)} custom-call(bf16[128,8192]{1,0:T(8,128)(2,1)} %bitcast.5, bf16[128,8192]{1,0:T(8,128)(2,1)} %bitcast.6, s32[1,128]{1,0:T(1,128)} %lw_hbm.1, s32[1,128]{1,0:T(1,128)} %docs_hbm.1, bf16[128,1024]{1,0:T(8,128)(2,1)} %bitcast.8, bf16[128,1024]{1,0:T(8,128)(2,1)} %bitcast.9, bf16[128,5120]{1,0:T(8,128)(2,1)} %bitcast.7, ...), custom_call_target="tpu_custom_call" | custom-call | flops 6006243328 | bytes 10000000 | tf_op jit(solution)/shard_map/layer_back/pallas_call | solution.py:668
  83.3 0.0 copy-done
  83.3 0.0 copy-done.1
  83.3 1.7 %add_divide_fusion = (f32[64,608]{1,0:T(8,128)}, f32[64,608]{1,0:T(8,128)}, f32[64,608]{1,0:T(8,128)}) fusion(f32[64,640]{1,0:T(8,128)} %layer_back.1, f32[64,608]{1,0:T(8,128)S(1)} %copy-done, f32[64,608]{1,0:T(8,128)S(1)} %copy-done.1), kind=kLoop, calls=%fused_computation.2 | loop fusion | flops 428032 | bytes 933888 | tf_op jit(solution)/shard_map/div | solution.py:717
Async XLA Ops:
  0.6 82.7 %copy-start = (f32[64,608]{1,0:T(8,128)S(1)}, f32[64,608]{1,0:T(8,128)}, u32[]{:S(2)}) copy-start(f32[64,608]{1,0:T(8,128)} %param.20) | copy-start | bytes 466948
  0.6 82.7 %copy-start.1 = (f32[64,608]{1,0:T(8,128)S(1)}, f32[64,608]{1,0:T(8,128)}, u32[]{:S(2)}) copy-start(f32[64,608]{1,0:T(8,128)} %param.19) | copy-start | bytes 466948

commit v3 on v2

--- a/solution.py
+++ b/solution.py
@@ -64,9 +64,9 @@
     q_hbm, g_hbm, lw_hbm, docs_hbm, k_hbm, v_hbm, x_hbm, a_hbm, table_hbm,
     out_ref,
     q_ref, g_ref, lw_ref, docs_ref, x_ref, a_ref, table,
-    kv_buf, back_buf, doc_buf, bias, lw_t, w_buf, dq_ref, dv_ref,
+    kv_buf, back_buf, doc_buf, bias, lw_t, w_buf, wt_buf, dq_ref, dv_ref,
     a_roll, z_in, f_ref,
-    grad, low_buf, mid_part, mid_buf, core_buf, stage, ry, rx, s2a, s2b, ry2, rx2,
+    grad, low_buf, low_q_ref, mid_part, mid_buf, core_out, core_buf, stage, ry, rx, s2a, s2b, ry2, rx2,
     total, z_out, rz, z_sum, full,
     in_sem, q_sem, g_sem, kv_sem, doc_send, doc_recv, send_sem, recv_sem, back_recv,
     fz_send, fz_recv, fx_send, fx_recv, fc_send, fc_recv,
@@ -217,10 +217,9 @@
         @pl.when(c + j < 8)
         def _():
             doc_copy(j).start()
-    lax.fori_loop(1, KV, send_own, 0)
+    send_own(1, 0)
 
     rank_rows = pl.ds(pl.multiple_of(core * HALF_ROWS, HALF_ROWS), HALF_ROWS)
-    block_cols = pl.ds(pl.multiple_of(x * XCOLS, HEAD), XCOLS)
     small[1].wait()
     a_roll[:, 512:WIN] = jnp.zeros((RANK, WIN - 512), F32)
     a_roll[:, 0:SHARD] = a_ref[...]
@@ -231,58 +230,73 @@
             a_roll[...] = pltpu.roll(a_roll[...], offsets[quarter], axis=1)
     z_in[z] = a_roll[rank_rows, :].astype(BF16)
 
-    def fz_copy(d):
-        return push(z_in.at[z], z_in.at[z], fz_send.at[d - 1], fz_recv.at[d - 1],
+    span = (slice(0, 16), slice(16, 32))
+
+    def fz_push(src, d, part):
+        return push(z_in.at[src, span[part]], z_in.at[src, span[part]],
+                    fz_send.at[part, d - 1], fz_recv.at[part, d - 1],
                     at(x, ahead(z, d, NZ), y, core))
 
-    def fz_wait(d):
-        src = ahead(z, NZ - d, NZ)
-        push(z_in.at[src], z_in.at[src], fz_send.at[d - 1], fz_recv.at[d - 1],
-             at(x, ahead(z, d, NZ), y, core)).wait_recv()
-
-    for d in range(1, NZ):
-        fz_copy(d).start()
-
-    def fx_copy(d):
-        return push(f_ref.at[rank_rows, block_cols], f_ref.at[rank_rows, block_cols],
-                    fx_send.at[d - 1], fx_recv.at[d - 1], at(ahead(x, d, NX), z, y, core))
+    for part in range(2):
+        for d in (4, 3, 5, 2, 6, 1, 7):
+            fz_push(z, d, part).start()
 
     def section(xx):
         return pl.ds(pl.multiple_of(xx * XCOLS, HEAD), XCOLS)
 
-    def fx_wait(d):
-        src = ahead(x, NX - d, NX)
-        push(f_ref.at[rank_rows, section(src)], f_ref.at[rank_rows, section(src)],
-             fx_send.at[d - 1], fx_recv.at[d - 1], at(ahead(x, d, NX), z, y, core)).wait_recv()
-
-    other_rows = pl.ds(pl.multiple_of((1 - core) * HALF_ROWS, HALF_ROWS), HALF_ROWS)
-
-    def fc_copy(d):
-        src = ahead(x, NX - d, NX)
-        return push(f_ref.at[rank_rows, section(src)], f_ref.at[rank_rows, section(src)],
-                    fc_send.at[d], fc_recv.at[d], at(x, z, y, 1 - core))
-
-    def fc_wait(d):
-        src = ahead(x, NX - d, NX)
-        push(f_ref.at[other_rows, section(src)], f_ref.at[other_rows, section(src)],
-             fc_send.at[d], fc_recv.at[d], at(x, z, y, 1 - core)).wait_recv()
-
-    def gather_block():
+    def half_section(xx, part):
+        return pl.ds(pl.multiple_of(xx * XCOLS + part * HALF, HEAD), HALF)
+
+    def f_rows(cc, part):
+        return pl.ds(pl.multiple_of(cc * HALF_ROWS + part * 16, 16), 16)
+
+    def fx_push(src, d, part):
+        where = f_ref.at[f_rows(core, part), section(src)]
+        return push(where, where, fx_send.at[part, d - 1], fx_recv.at[part, d - 1],
+                    at(ahead(x, d, NX), z, y, core))
+
+    def fc_push(cc, d, part):
+        where = f_ref.at[f_rows(cc, part), section(ahead(x, NX - d, NX))]
+        return push(where, where, fc_send.at[part, d], fc_recv.at[part, d],
+                    at(x, z, y, 1 - core))
+
+    def gather_block(part):
         for d in range(1, NZ):
-            fz_wait(d)
+            fz_push(ahead(z, NZ - d, NZ), d, part).wait_recv()
         for quad in range(2):
-            w = [z_in[quad * 4 + i] for i in range(4)]
+            w = [z_in[quad * 4 + i, span[part]] for i in range(4)]
             pieces = [
                 w[0][:, 0:512], w[0][:, 512:640] + w[1][:, 0:128],
                 w[1][:, 128:640], w[1][:, 640:768] + w[2][:, 0:128],
                 w[2][:, 128:640], w[2][:, 640:768] + w[3][:, 0:128],
                 w[3][:, 128:640],
             ]
-            where = pl.ds(pl.multiple_of(x * XCOLS + quad * HALF, HEAD), HALF)
-            f_ref[rank_rows, where] = jnp.concatenate(pieces, axis=1)
-        for d in range(1, NX):
-            fx_copy(d).start()
-        fc_copy(0).start()
+            f_ref[f_rows(core, part), half_section(x, quad)] = jnp.concatenate(pieces, axis=1)
+        for d in (2, 1, 3):
+            fx_push(x, d, part).start()
+        fc_push(core, 0, part).start()
+
+    def gather_pair(part):
+        for d in (1, 3, 2):
+            fx_push(ahead(x, NX - d, NX), d, part).wait_recv()
+            fc_push(core, d, part).start()
+
+    def low_copy(j):
+        return push(low_buf.at[own], low_buf.at[own - j], low_send.at[j - 1],
+                    low_recv.at[own - j], (dp, c + j))
+
+    def make_low():
+        for part in range(2):
+            for d in range(NX):
+                fc_push(1 - core, d, part).wait_recv()
+        small[4].wait()
+        both = dot(jnp.concatenate([f_ref[:, D:2 * D], f_ref[:, 0:D]], axis=0), x_ref[...], NT)
+        low_buf[own] = both[0:RANK].astype(BF16)
+        for j in range(1, BLOCKS):
+            @pl.when(c + j < 8)
+            def _():
+                low_copy(j).start()
+        low_q_ref[...] = both[RANK:].astype(BF16)
 
     def relay_near(h):
         @pl.when(y >= 1)
@@ -324,10 +338,26 @@
         def _():
             pair_far_down(h).wait_recv()
 
-    relay_near(0)
-    relay_near(1)
     small[2].wait()
     lw_t[...] = jnp.broadcast_to(lw_ref[...].astype(F32), (ROWS, ROWS)).T
+
+    def weigh(h, carry):
+        g_load(h).wait()
+        weighted = [
+            (g_ref[:, pl.ds(pl.multiple_of(h * 1024 + i * HEAD, HEAD), HEAD)].astype(F32)
+             * lw_t[...]).astype(BF16)
+            for i in range(GROUP)]
+        for i in range(GROUP):
+            w_buf[h, i * ROWS:(i + 1) * ROWS] = weighted[i]
+            wt_buf[h, :, i * ROWS:(i + 1) * ROWS] = turn(weighted[i])
+        return carry
+
+    lax.fori_loop(0, 3, weigh, 0)
+    relay_near(0)
+    send_own(2, 0)
+    relay_near(1)
+    send_own(3, 0)
+    lax.fori_loop(3, KV, weigh, 0)
     for slot in range(own):
         @pl.when(c + slot >= own)
         def _():
@@ -337,9 +367,13 @@
     key_pos = lax.broadcasted_iota(jnp.int32, (ROWS, ROWS), 1)
     for slot in range(BLOCKS):
         allowed = jnp.broadcast_to(doc_buf[slot][0:1, :], (ROWS, ROWS)) == doc_col
-        if slot == own:
-            allowed = jnp.logical_and(allowed, key_pos <= row_pos)
-        bias[:, slot * ROWS:(slot + 1) * ROWS] = jnp.where(allowed, 0.0, NEG)
+        block = jnp.where(allowed, 0.0, NEG)
+        if slot == 0:
+            first_block = block
+        elif slot == own:
+            bias[:, 0:ROWS] = jnp.where(key_pos <= row_pos, block, first_block)
+        else:
+            bias[:, slot * ROWS:(slot + 1) * ROWS] = block
     small[3].wait()
     relay_far(0)
 
@@ -347,21 +381,51 @@
     fold = scale * float(np.log2(np.e))
     part_heads = 4
 
+    edge = own * ROWS
+
     def one_group(h, carry):
+        lower = lax.broadcasted_iota(jnp.int32, (ROWS, ROWS), 1) <= lax.broadcasted_iota(
+            jnp.int32, (ROWS, ROWS), 0)
+
+        def fold_ends(a):
+            return jnp.concatenate(
+                [jnp.where(lower, a[:, edge:], a[:, 0:ROWS]), a[:, ROWS:edge]], axis=1)
+
+        def unfold_ends(a):
+            ends = a[:, 0:ROWS]
+            return jnp.concatenate(
+                [jnp.where(lower, 0.0, ends).astype(BF16), a[:, ROWS:].astype(BF16),
+                 jnp.where(lower, ends, 0.0).astype(BF16)], axis=1)
+
         @pl.when(h + 2 < KV)
         def _():
             relay_near(h + 2)
 
+        @pl.when(h + 4 < KV)
+        def _():
+            send_own(h + 4, 0)
+
         @pl.when(h + 1 < KV)
         def _():
             relay_far(h + 1)
 
+        @pl.when(h == 1)
+        def _():
+            gather_block(0)
+
         @pl.when(h == 2)
         def _():
-            gather_block()
+            gather_block(1)
+
+        @pl.when(h == 5)
+        def _():
+            gather_pair(0)
+
+        @pl.when(h == 7)
+        def _():
+            gather_pair(1)
 
         q_load(h).wait()
-        g_load(h).wait()
         arrive(h)
         keys = kv_buf[h, :, 0].reshape(WINDOW, HEAD)
         vals = kv_buf[h, :, 1].reshape(WINDOW, HEAD)
@@ -372,10 +436,7 @@
         def front(part):
             heads = range(part * part_heads, (part + 1) * part_heads)
             queries = jnp.concatenate([q_ref[:, head_cols(i)] for i in heads], axis=0)
-            weighted = jnp.concatenate(
-                [(g_ref[:, head_cols(i)].astype(F32) * lw_t[...]).astype(BF16) for i in heads],
-                axis=0)
-            w_buf[part] = weighted
+            weighted = w_buf[h, part * 512:(part + 1) * 512]
             return dot(queries, keys, NT), dot(weighted, vals, NT)
 
         parts = GROUP // part_heads
@@ -388,46 +449,32 @@
             probs_b, dscores = [], []
             for t in range(part_heads):
                 rows = slice(t * ROWS, (t + 1) * ROWS)
-                masked = scores[rows] + bias[...]
+                masked = fold_ends(scores[rows]) + bias[...]
                 top = jnp.max(masked, axis=1, keepdims=True)
                 expo = jnp.exp2((masked - top) * fold)
                 probs = expo * (1.0 / jnp.sum(expo, axis=1, keepdims=True))
-                dp_rows = dprobs[rows]
+                dp_rows = fold_ends(dprobs[rows])
                 delta = jnp.sum(probs * dp_rows, axis=1, keepdims=True)
-                probs_b.append(probs.astype(BF16))
-                dscores.append((probs * (dp_rows - delta)).astype(BF16))
+                probs_b.append(unfold_ends(probs))
+                dscores.append(unfold_ends(probs * (dp_rows - delta)))
             dq = dot(jnp.concatenate(dscores, axis=0), keys, NN) * scale
             for t in range(part_heads):
                 rot = dq[t * ROWS:(t + 1) * ROWS].astype(BF16).astype(F32)
                 dq_ref[:, head_cols(part * part_heads + t)] = (
                     rot * table[0] + pltpu.roll(rot, HEAD // 2, axis=1) * table[1]).astype(BF16)
-            more = dot(turn(w_buf[part]), jnp.concatenate(probs_b, axis=0), NN)
+            more = dot(
+                wt_buf[h, :, part * 512:(part + 1) * 512], jnp.concatenate(probs_b, axis=0), NN)
             dv = more if dv is None else dv + more
         dv_ref[cols_of(h, HEAD), :] = dv.astype(BF16)
         return carry
 
     lax.fori_loop(0, KV, one_group, 0)
-
-    for d in range(1, NX):
-        fx_wait(d)
-        fc_copy(d).start()
-    small[4].wait()
-    for d in range(NX):
-        fc_wait(d)
-
-    def low_copy(j):
-        return push(low_buf.at[own], low_buf.at[own - j], low_send.at[j - 1],
-                    low_recv.at[own - j], (dp, c + j))
+    make_low()
 
     def mid_copy(j):
         return push(mid_part.at[own - j], mid_buf.at[j - 1], mid_send.at[j - 1],
                     mid_recv.at[j - 1], (dp, c - j))
 
-    low_buf[own] = dot(f_ref[:, D:2 * D], x_ref[...], NT).astype(BF16)
-    for j in range(1, BLOCKS):
-        @pl.when(c + j < 8)
-        def _():
-            low_copy(j).start()
     piece = dot(f_ref[:, BV:FACT], dv_ref[...], NN)
     for slot in range(BLOCKS):
         mid_part[slot] = piece[:, slot * ROWS:(slot + 1) * ROWS]
@@ -436,41 +483,15 @@
         def _():
             mid_copy(j).start()
 
-    low_q = dot(f_ref[:, 0:D], x_ref[...], NT).astype(BF16)
-    for i in range(KV):
-        grad[:, BQ + i * 1024:BQ + (i + 1) * 1024] = dot(
-            low_q, dq_ref[:, i * 1024:(i + 1) * 1024], NN)
-    for slot in range(own):
-        @pl.when(c + slot >= own)
-        def _():
-            low_copy(own - slot).wait_recv()
-    low_window = jnp.concatenate([low_buf[s] for s in range(BLOCKS)], axis=1)
-    grad[:, BV:FACT] = dot(low_window, dv_ref[...], NT)
-
     def core_copy(part_x):
-        return push(
-            grad.at[:, pl.ds(pl.multiple_of(part_x * XCOLS + (1 - core) * HALF, HEAD), HALF)],
-            core_buf.at[part_x], core_send.at[part_x], core_recv.at[part_x],
-            at(x, z, y, 1 - core))
-
-    core_copy(3).start()
-    mid_q = dot(f_ref[:, BQ:BV], dq_ref[...], NT).astype(BF16)
-    for i in range(5):
-        cols = slice(i * 1024, (i + 1) * 1024)
-        grad[:, cols] = dot(mid_q, x_ref[:, cols], NN)
-    core_copy(0).start()
-    mid_v = mid_part[own]
-    for j in range(1, BLOCKS):
-        @pl.when(c + j < 8)
-        def _():
-            mid_copy(j).wait_recv()
-        mid_v = mid_v + mid_buf[j - 1]
-    mid_v = mid_v.astype(BF16)
-    for i in range(5):
-        grad[:, D + i * 1024:D + (i + 1) * 1024] = dot(
-            mid_v, x_ref[:, i * 1024:(i + 1) * 1024], NN)
-    core_copy(1).start()
-    core_copy(2).start()
+        return push(core_out.at[part_x], core_buf.at[part_x], core_send.at[part_x],
+                    core_recv.at[part_x], at(x, z, y, 1 - core))
+
+    def core_start(part_x):
+        theirs = grad[:, pl.ds(
+            pl.multiple_of(part_x * XCOLS + (1 - core) * HALF, HEAD), HALF)]
+        core_out[part_x] = theirs.astype(BF16)
+        core_copy(part_x).start()
 
     def y_rows(yy):
         return pl.ds(pl.multiple_of(yy * 16, 16), 16)
@@ -485,17 +506,54 @@
         return push(stage.at[xx, :, CUT:HALF], rx.at[d - 1],
                     x_send.at[d - 1], x_recv.at[d - 1], at(xx, z, y, core))
 
-    for part_x in (3, 0, 1, 2):
+    def core_finish(part_x):
         core_copy(part_x).wait_recv()
         mine = grad[:, pl.ds(pl.multiple_of(part_x * XCOLS + core * HALF, HEAD), HALF)]
-        stage[part_x] = (mine + core_buf[part_x]).astype(BF16)
-        for d in range(1, NY):
+        stage[part_x] = (mine + core_buf[part_x].astype(F32)).astype(BF16)
+        for d in (2, 1, 3):
             y_copy(d, part_x).start()
         for d in range(1, NX):
             @pl.when(ahead(x, d, NX) == part_x)
             def _():
                 x_copy(d).start()
 
+    def q_rank_cols(first, last):
+        for i in range(first, last, 1024):
+            stop = min(i + 1024, last)
+            grad[:, BQ + i:BQ + stop] = dot(low_q_ref[...], dq_ref[:, i:stop], NN)
+
+    q_cut = 3 * XCOLS - BQ
+    mid_q = dot(f_ref[:, BQ:BV], dq_ref[...], NT).astype(BF16)
+    for i in range(5):
+        grad[:, i * 1024:(i + 1) * 1024] = dot(mid_q, x_ref[:, i * 1024:(i + 1) * 1024], NN)
+    core_start(0)
+    q_rank_cols(q_cut, QW)
+    for slot in range(own):
+        @pl.when(c + slot >= own)
+        def _():
+            low_copy(own - slot).wait_recv()
+    low_window = jnp.concatenate([low_buf[s] for s in range(BLOCKS)], axis=1)
+    grad[:, BV:FACT] = dot(low_window, dv_ref[...], NT)
+    core_start(3)
+    core_finish(0)
+    q_rank_cols(0, q_cut)
+    mid_v = mid_part[own]
+    for j in range(1, BLOCKS):
+        @pl.when(c + j < 8)
+        def _():
+            mid_copy(j).wait_recv()
+        mid_v = mid_v + mid_buf[j - 1]
+    mid_v = mid_v.astype(BF16)
+    for i in (4, 3, 2, 1, 0):
+        grad[:, D + i * 1024:D + (i + 1) * 1024] = dot(
+            mid_v, x_ref[:, i * 1024:(i + 1) * 1024], NN)
+        if i == 4:
+            core_start(2)
+    core_start(1)
+    core_finish(3)
+    core_finish(2)
+    core_finish(1)
+
     def x2_copy(d):
         return push(s2a.at[d - 1], rx2.at[d - 1], x2_send.at[d - 1], x2_recv.at[d - 1],
                     at(ahead(x, d, NX), z, y, core))
@@ -504,19 +562,23 @@
         return push(s2b.at[d - 1], ry2.at[d - 1], y2_send.at[d - 1], y2_recv.at[d - 1],
                     at(x, z, ahead(y, d, NY), core))
 
-    for part_x in (3, 0, 1, 2):
+    for part_x in (0, 3, 2, 1):
         for d in range(1, NY):
             y_copy(d, part_x).wait_recv()
-    for d in (1, 2, 3, 0):
-        xx = ahead(x, d, NX)
-        value = stage[xx, y_rows(y), 0:CUT].astype(F32)
+        value = stage[part_x, y_rows(y), 0:CUT].astype(F32)
         for e in range(NY - 1):
-            value = value + ry[e, xx].astype(F32)
-        if d:
-            s2a[d - 1] = value.astype(BF16)
-            x2_copy(d).start()
-        else:
+            value = value + ry[e, part_x].astype(F32)
+
+        @pl.when(x == part_x)
+        def _():
             total[:, 0:CUT] = value
+
+        for d in range(1, NX):
+            @pl.when(ahead(x, d, NX) == part_x)
+            def _():
+                s2a[d - 1] = value.astype(BF16)
+                x2_copy(d).start()
+
     for d in range(1, NX):
         x_copy(d).wait_recv()
     for d in (1, 2, 3, 0):
@@ -636,12 +698,13 @@
         return carry
 
     lax.fori_loop(0, KV, drain, 0)
-    for d in range(1, NZ):
-        fz_copy(d).wait_send()
-    for d in range(1, NX):
-        fx_copy(d).wait_send()
-    for d in range(NX):
-        fc_copy(d).wait_send()
+    for part in range(2):
+        for d in range(1, NZ):
+            fz_push(z, d, part).wait_send()
+        for d in range(1, NX):
+            fx_push(x, d, part).wait_send()
+        for d in range(NX):
+            fc_push(core, d, part).wait_send()
     for part_x in range(NX):
         core_copy(part_x).wait_send()
         for d in range(1, NY):
@@ -675,13 +738,13 @@
             mem((1, ROWS), jnp.int32), mem((1, ROWS), jnp.int32),
             mem((ROWS, D), BF16), mem((RANK, SHARD), F32), mem((2, ROWS, HEAD), F32),
             mem((KV, BLOCKS, 2, ROWS, HEAD), BF16), mem((KV, 2, ROWS, HEAD), BF16),
-            mem((BLOCKS, 8, ROWS), F32), mem((ROWS, WINDOW), F32), mem((ROWS, ROWS), F32),
-            mem((2, 4 * ROWS, HEAD), BF16),
+            mem((BLOCKS, 8, ROWS), F32), mem((ROWS, WINDOW - ROWS), F32), mem((ROWS, ROWS), F32),
+            mem((KV, GROUP * ROWS, HEAD), BF16), mem((KV, HEAD, GROUP * ROWS), BF16),
             mem((ROWS, QW), BF16), mem((KV * HEAD, WINDOW), BF16),
             mem((RANK, WIN), F32), mem((NZ, HALF_ROWS, WIN), BF16), mem((RANK, FACT), BF16),
-            mem((RANK, FACT), F32), mem((BLOCKS, RANK, ROWS), BF16),
+            mem((RANK, FACT), F32), mem((BLOCKS, RANK, ROWS), BF16), mem((RANK, ROWS), BF16),
             mem((BLOCKS, RANK, ROWS), F32), mem((BLOCKS - 1, RANK, ROWS), F32),
-            mem((NX, RANK, HALF), F32), mem((NX, RANK, HALF), BF16),
+            mem((NX, RANK, HALF), BF16), mem((NX, RANK, HALF), BF16), mem((NX, RANK, HALF), BF16),
             mem((NY - 1, NX, 16, CUT), BF16), mem((NX - 1, RANK, REST), BF16),
             mem((NX - 1, 16, CUT), BF16), mem((NY - 1, 16, REST), BF16),
             mem((NY - 1, 16, REST), BF16), mem((NX - 1, 16, CUT), BF16),
@@ -689,7 +752,7 @@
             mem((16, WIN), F32), mem((RANK, 640), F32),
             dma((5,)), dma((KV,)), dma((KV,)), dma((KV, 2)), dma((4,)), dma((4,)),
             dma((KV, 7)), dma((KV, 4)), dma((KV,)),
-            dma((7,)), dma((7,)), dma((3,)), dma((3,)), dma((4,)), dma((4,)),
+            dma((2, 7)), dma((2, 7)), dma((2, 3)), dma((2, 3)), dma((2, 4)), dma((2, 4)),
             dma((4,)), dma((4,)), dma((4,)), dma((4,)), dma((4,)), dma((4,)),
             dma((3, 4)), dma((3, 4)), dma((3,)), dma((3,)),
             dma((3,)), dma((3,)), dma((3,)), dma((3,)),

time: 85.2 us -> 75.4 us (0.88)
  the two profiles are of different devices: /device:TPU:1 before, /device:TPU:3 now
where the time goes in v3:
time: 75.4 us; the launch traced here: 75.2 us
  Pallas kernels  72.8 us (97%)
  other arithmetic  1.74 us (2%)
    pallas_call x1, Pallas kernels, reduced_gradient(): pl.pallas_call(kernel, out_shape=jax.ShapeDtypeStruct((RANK, 640), F32),...  72.8 us
    div x1, other arithmetic, per_device(): new_m / corr_one / (jnp.sqrt(new_v / corr_two) + ADAM_EPS)  1.74 us

profile of v3, /device:TPU:3, one launch (start us, length us, event | category | flops | bytes accessed | tf_op | source)
XLA Modules:
  0.0 75.2 jit_solution(2823848315244944527)
XLA Ops:
  0.6 0.0 copy-start
  0.6 0.0 copy-start.1
  0.7 72.8 %layer_back.1 = f32[64,640]{1,0:T(8,128)} custom-call(bf16[128,8192]{1,0:T(8,128)(2,1)} %bitcast.5, bf16[128,8192]{1,0:T(8,128)(2,1)} %bitcast.6, s32[1,128]{1,0:T(1,128)} %lw_hbm.1, s32[1,128]{1,0:T(1,128)} %docs_hbm.1, bf16[128,1024]{1,0:T(8,128)(2,1)} %bitcast.8, bf16[128,1024]{1,0:T(8,128)(2,1)} %bitcast.9, bf16[128,5120]{1,0:T(8,128)(2,1)} %bitcast.7, ...), custom_call_target="tpu_custom_call" | custom-call | flops 6006243328 | bytes 10000000 | tf_op jit(solution)/shard_map/layer_back/pallas_call | solution.py:731
  73.5 0.0 copy-done
  73.5 0.0 copy-done.1
  73.5 1.7 %add_divide_fusion = (f32[64,608]{1,0:T(8,128)}, f32[64,608]{1,0:T(8,128)}, f32[64,608]{1,0:T(8,128)}) fusion(f32[64,640]{1,0:T(8,128)} %layer_back.1, f32[64,608]{1,0:T(8,128)S(1)} %copy-done, f32[64,608]{1,0:T(8,128)S(1)} %copy-done.1), kind=kLoop, calls=%fused_computation.2 | loop fusion | flops 428032 | bytes 933888 | tf_op jit(solution)/shard_map/div | solution.py:780
Async XLA Ops:
  0.6 72.9 %copy-start = (f32[64,608]{1,0:T(8,128)S(1)}, f32[64,608]{1,0:T(8,128)}, u32[]{:S(2)}) copy-start(f32[64,608]{1,0:T(8,128)} %param.20) | copy-start | bytes 466948
  0.6 72.9 %copy-start.1 = (f32[64,608]{1,0:T(8,128)S(1)}, f32[64,608]{1,0:T(8,128)}, u32[]{:S(2)}) copy-start(f32[64,608]{1,0:T(8,128)} %param.19) | copy-start | bytes 466948

commit v4 on v3

--- a/solution.py
+++ b/solution.py
@@ -25,7 +25,7 @@
 XCOLS = FACT // NX
 HALF = XCOLS // 2
 HALF_ROWS = RANK // 2
-CUT = 1152
+CUT = 1408
 REST = HALF - CUT
 WIN = 768
 
@@ -64,7 +64,7 @@
     q_hbm, g_hbm, lw_hbm, docs_hbm, k_hbm, v_hbm, x_hbm, a_hbm, table_hbm,
     out_ref,
     q_ref, g_ref, lw_ref, docs_ref, x_ref, a_ref, table,
-    kv_buf, back_buf, doc_buf, bias, lw_t, w_buf, wt_buf, dq_ref, dv_ref,
+    kv_buf, back_buf, doc_buf, bias, lw_t, w_buf, dq_ref, dv_ref,
     a_roll, z_in, f_ref,
     grad, low_buf, low_q_ref, mid_part, mid_buf, core_out, core_buf, stage, ry, rx, s2a, s2b, ry2, rx2,
     total, z_out, rz, z_sum, full,
@@ -341,23 +341,10 @@
     small[2].wait()
     lw_t[...] = jnp.broadcast_to(lw_ref[...].astype(F32), (ROWS, ROWS)).T
 
-    def weigh(h, carry):
-        g_load(h).wait()
-        weighted = [
-            (g_ref[:, pl.ds(pl.multiple_of(h * 1024 + i * HEAD, HEAD), HEAD)].astype(F32)
-             * lw_t[...]).astype(BF16)
-            for i in range(GROUP)]
-        for i in range(GROUP):
-            w_buf[h, i * ROWS:(i + 1) * ROWS] = weighted[i]
-            wt_buf[h, :, i * ROWS:(i + 1) * ROWS] = turn(weighted[i])
-        return carry
-
-    lax.fori_loop(0, 3, weigh, 0)
     relay_near(0)
     send_own(2, 0)
     relay_near(1)
     send_own(3, 0)
-    lax.fori_loop(3, KV, weigh, 0)
     for slot in range(own):
         @pl.when(c + slot >= own)
         def _():
@@ -375,6 +362,8 @@
         else:
             bias[:, slot * ROWS:(slot + 1) * ROWS] = block
     small[3].wait()
+    relay_near(2)
+    send_own(4, 0)
     relay_far(0)
 
     scale = 1.0 / HEAD ** 0.5
@@ -397,35 +386,40 @@
                 [jnp.where(lower, 0.0, ends).astype(BF16), a[:, ROWS:].astype(BF16),
                  jnp.where(lower, ends, 0.0).astype(BF16)], axis=1)
 
-        @pl.when(h + 2 < KV)
-        def _():
-            relay_near(h + 2)
-
-        @pl.when(h + 4 < KV)
-        def _():
-            send_own(h + 4, 0)
+        @pl.when(h + 3 < KV)
+        def _():
+            relay_near(h + 3)
+
+        @pl.when(h + 5 < KV)
+        def _():
+            send_own(h + 5, 0)
 
         @pl.when(h + 1 < KV)
         def _():
             relay_far(h + 1)
 
+        @pl.when(h == 0)
+        def _():
+            gather_block(0)
+
         @pl.when(h == 1)
         def _():
-            gather_block(0)
-
-        @pl.when(h == 2)
-        def _():
             gather_block(1)
 
-        @pl.when(h == 5)
+        @pl.when(h == 4)
         def _():
             gather_pair(0)
 
-        @pl.when(h == 7)
+        @pl.when(h == 6)
         def _():
             gather_pair(1)
 
+        @pl.when(h == KV - 1)
+        def _():
+            make_low()
+
         q_load(h).wait()
+        g_load(h).wait()
         arrive(h)
         keys = kv_buf[h, :, 0].reshape(WINDOW, HEAD)
         vals = kv_buf[h, :, 1].reshape(WINDOW, HEAD)
@@ -436,7 +430,10 @@
         def front(part):
             heads = range(part * part_heads, (part + 1) * part_heads)
             queries = jnp.concatenate([q_ref[:, head_cols(i)] for i in heads], axis=0)
-            weighted = w_buf[h, part * 512:(part + 1) * 512]
+            weighted = jnp.concatenate(
+                [(g_ref[:, head_cols(i)].astype(F32) * lw_t[...]).astype(BF16) for i in heads],
+                axis=0)
+            w_buf[part] = weighted
             return dot(queries, keys, NT), dot(weighted, vals, NT)
 
         parts = GROUP // part_heads
@@ -463,13 +460,12 @@
                 dq_ref[:, head_cols(part * part_heads + t)] = (
                     rot * table[0] + pltpu.roll(rot, HEAD // 2, axis=1) * table[1]).astype(BF16)
             more = dot(
-                wt_buf[h, :, part * 512:(part + 1) * 512], jnp.concatenate(probs_b, axis=0), NN)
+                turn(w_buf[part]), jnp.concatenate(probs_b, axis=0), NN)
             dv = more if dv is None else dv + more
         dv_ref[cols_of(h, HEAD), :] = dv.astype(BF16)
         return carry
 
     lax.fori_loop(0, KV, one_group, 0)
-    make_low()
 
     def mid_copy(j):
         return push(mid_part.at[own - j], mid_buf.at[j - 1], mid_send.at[j - 1],
@@ -517,26 +513,22 @@
             def _():
                 x_copy(d).start()
 
-    def q_rank_cols(first, last):
-        for i in range(first, last, 1024):
-            stop = min(i + 1024, last)
-            grad[:, BQ + i:BQ + stop] = dot(low_q_ref[...], dq_ref[:, i:stop], NN)
-
-    q_cut = 3 * XCOLS - BQ
+    for i in range(KV):
+        grad[:, BQ + i * 1024:BQ + (i + 1) * 1024] = dot(
+            low_q_ref[...], dq_ref[:, i * 1024:(i + 1) * 1024], NN)
+    core_start(2 + core)
     mid_q = dot(f_ref[:, BQ:BV], dq_ref[...], NT).astype(BF16)
     for i in range(5):
         grad[:, i * 1024:(i + 1) * 1024] = dot(mid_q, x_ref[:, i * 1024:(i + 1) * 1024], NN)
     core_start(0)
-    q_rank_cols(q_cut, QW)
+    core_finish(3 - core)
     for slot in range(own):
         @pl.when(c + slot >= own)
         def _():
             low_copy(own - slot).wait_recv()
     low_window = jnp.concatenate([low_buf[s] for s in range(BLOCKS)], axis=1)
     grad[:, BV:FACT] = dot(low_window, dv_ref[...], NT)
-    core_start(3)
     core_finish(0)
-    q_rank_cols(0, q_cut)
     mid_v = mid_part[own]
     for j in range(1, BLOCKS):
         @pl.when(c + j < 8)
@@ -548,10 +540,9 @@
         grad[:, D + i * 1024:D + (i + 1) * 1024] = dot(
             mid_v, x_ref[:, i * 1024:(i + 1) * 1024], NN)
         if i == 4:
-            core_start(2)
+            core_start(3 - core)
     core_start(1)
-    core_finish(3)
-    core_finish(2)
+    core_finish(2 + core)
     core_finish(1)
 
     def x2_copy(d):
@@ -562,7 +553,7 @@
         return push(s2b.at[d - 1], ry2.at[d - 1], y2_send.at[d - 1], y2_recv.at[d - 1],
                     at(x, z, ahead(y, d, NY), core))
 
-    for part_x in (0, 3, 2, 1):
+    for part_x in (3 - core, 0, 2 + core, 1):
         for d in range(1, NY):
             y_copy(d, part_x).wait_recv()
         value = stage[part_x, y_rows(y), 0:CUT].astype(F32)
@@ -638,7 +629,7 @@
             def _():
                 shift = quarter * SHARD - starts[quarter]
                 moved = pltpu.roll(value, WIN - shift, axis=1) if shift else value
-                full[y_rows(y), :] = moved[:, 0:640]
+                full[y_rows(y), :] = moved[:, 0:640].astype(BF16)
         for j in range(1, 8):
             full_copy(j).start()
 
@@ -655,7 +646,7 @@
     def _():
         row_wait(y)
 
-    out_ref[...] = full[...] * (ADAPTER_SCALE / (NX * NZ))
+    out_ref[...] = full[...].astype(F32) * (ADAPTER_SCALE / (NX * NZ))
 
     for j in range(1, BLOCKS):
         @pl.when(c + j < 8)
@@ -739,7 +730,7 @@
             mem((ROWS, D), BF16), mem((RANK, SHARD), F32), mem((2, ROWS, HEAD), F32),
             mem((KV, BLOCKS, 2, ROWS, HEAD), BF16), mem((KV, 2, ROWS, HEAD), BF16),
             mem((BLOCKS, 8, ROWS), F32), mem((ROWS, WINDOW - ROWS), F32), mem((ROWS, ROWS), F32),
-            mem((KV, GROUP * ROWS, HEAD), BF16), mem((KV, HEAD, GROUP * ROWS), BF16),
+            mem((2, 4 * ROWS, HEAD), BF16),
             mem((ROWS, QW), BF16), mem((KV * HEAD, WINDOW), BF16),
             mem((RANK, WIN), F32), mem((NZ, HALF_ROWS, WIN), BF16), mem((RANK, FACT), BF16),
             mem((RANK, FACT), F32), mem((BLOCKS, RANK, ROWS), BF16), mem((RANK, ROWS), BF16),
@@ -749,7 +740,7 @@
             mem((NX - 1, 16, CUT), BF16), mem((NY - 1, 16, REST), BF16),
             mem((NY - 1, 16, REST), BF16), mem((NX - 1, 16, CUT), BF16),
             mem((16, HALF), F32), mem((16, HALF), BF16), mem((NZ, 16, WIN), BF16),
-            mem((16, WIN), F32), mem((RANK, 640), F32),
+            mem((16, WIN), F32), mem((RANK, 640), BF16),
             dma((5,)), dma((KV,)), dma((KV,)), dma((KV, 2)), dma((4,)), dma((4,)),
             dma((KV, 7)), dma((KV, 4)), dma((KV,)),
             dma((2, 7)), dma((2, 7)), dma((2, 3)), dma((2, 3)), dma((2, 4)), dma((2, 4)),

time: 75.4 us -> 71.4 us (0.947)
  the two profiles are of different devices: /device:TPU:3 before, /device:TPU:1 now
where the time goes in v4:
time: 71.4 us; the launch traced here: 71.3 us
  Pallas kernels  68.9 us (96%)
  other arithmetic  1.74 us (2%)
    pallas_call x1, Pallas kernels, reduced_gradient(): pl.pallas_call(kernel, out_shape=jax.ShapeDtypeStruct((RANK, 640), F32),...  68.9 us
    div x1, other arithmetic, per_device(): new_m / corr_one / (jnp.sqrt(new_v / corr_two) + ADAM_EPS)  1.74 us

profile of v4, /device:TPU:1, one launch (start us, length us, event | category | flops | bytes accessed | tf_op | source)
XLA Modules:
  0.0 71.3 jit_solution(18169210957726126243)
XLA Ops:
  0.6 0.0 copy-start
  0.6 0.0 copy-start.1
  0.7 68.9 %layer_back.1 = f32[64,640]{1,0:T(8,128)} custom-call(bf16[128,8192]{1,0:T(8,128)(2,1)} %bitcast.5, bf16[128,8192]{1,0:T(8,128)(2,1)} %bitcast.6, s32[1,128]{1,0:T(1,128)} %lw_hbm.1, s32[1,128]{1,0:T(1,128)} %docs_hbm.1, bf16[128,1024]{1,0:T(8,128)(2,1)} %bitcast.8, bf16[128,1024]{1,0:T(8,128)(2,1)} %bitcast.9, bf16[128,5120]{1,0:T(8,128)(2,1)} %bitcast.7, ...), custom_call_target="tpu_custom_call" | custom-call | flops 6006243328 | bytes 10000000 | tf_op jit(solution)/shard_map/layer_back/pallas_call | solution.py:722
  69.5 0.0 copy-done
  69.5 0.0 copy-done.1
  69.5 1.7 %add_divide_fusion = (f32[64,608]{1,0:T(8,128)}, f32[64,608]{1,0:T(8,128)}, f32[64,608]{1,0:T(8,128)}) fusion(f32[64,640]{1,0:T(8,128)} %layer_back.1, f32[64,608]{1,0:T(8,128)S(1)} %copy-done, f32[64,608]{1,0:T(8,128)S(1)} %copy-done.1), kind=kLoop, calls=%fused_computation.2 | loop fusion | flops 428032 | bytes 933888 | tf_op jit(solution)/shard_map/div | solution.py:771
Async XLA Ops:
  0.6 68.9 %copy-start = (f32[64,608]{1,0:T(8,128)S(1)}, f32[64,608]{1,0:T(8,128)}, u32[]{:S(2)}) copy-start(f32[64,608]{1,0:T(8,128)} %param.20) | copy-start | bytes 466948
  0.6 68.9 %copy-start.1 = (f32[64,608]{1,0:T(8,128)S(1)}, f32[64,608]{1,0:T(8,128)}, u32[]{:S(2)}) copy-start(f32[64,608]{1,0:T(8,128)} %param.19) | copy-start | bytes 466948

commit v5 on v4

--- a/solution.py
+++ b/solution.py
@@ -154,71 +154,6 @@
 
     small[0].wait()
     doc_buf[own] = jnp.broadcast_to(docs_ref[...].astype(F32), (8, ROWS))
-    pl.semaphore_wait(barrier, len(peers))
-
-    def doc_copy(j):
-        return push(doc_buf.at[own], doc_buf.at[own - j], doc_send.at[j - 1],
-                    doc_recv.at[own - j], (dp, c + j))
-
-    def kv_copy(h, kind, source, target, peer):
-        return push(kv_buf.at[h, source], kv_buf.at[h, target], send_sem.at[h, kind],
-                    recv_sem.at[h, target], (dp, peer))
-
-    def hop_own(h):
-        return kv_copy(h, 0, 4, 2, c + 2)
-
-    def pair_own(h):
-        return kv_copy(h, 1, 4, 3, c + 1)
-
-    def hop_relay(h):
-        return kv_copy(h, 2, 2, 0, c + 2)
-
-    def pair_near_up(h):
-        return kv_copy(h, 3, 2, 1, c + 1)
-
-    def pair_near_down(h):
-        return kv_copy(h, 3, 2, 3, c - 1)
-
-    def pair_far_down(h):
-        return kv_copy(h, 4, 0, 1, c - 1)
-
-    def back_own(h):
-        return push(kv_buf.at[h, own], back_buf.at[h], send_sem.at[h, 5], back_recv.at[h],
-                    (dp, ahead(c, 6, 8)))
-
-    def back_relay(h):
-        return push(back_buf.at[h], kv_buf.at[h, 0], send_sem.at[h, 6], recv_sem.at[h, 0],
-                    (dp, ahead(c, 6, 8)))
-
-    def is_back(h):
-        return h % 2 == 1
-
-    outer = jnp.logical_or(y == 0, y == 3)
-
-    def send_own(h, carry):
-        kv_load(h, 0).wait()
-        kv_load(h, 1).wait()
-
-        @pl.when(y < 3)
-        def _():
-            hop_own(h).start()
-
-        @pl.when(core == 0)
-        def _():
-            pair_own(h).start()
-
-        @pl.when(jnp.logical_and(is_back(h), y < 2))
-        def _():
-            back_own(h).start()
-        return carry
-
-    send_own(0, 0)
-    for j in range(1, BLOCKS):
-        @pl.when(c + j < 8)
-        def _():
-            doc_copy(j).start()
-    send_own(1, 0)
-
     rank_rows = pl.ds(pl.multiple_of(core * HALF_ROWS, HALF_ROWS), HALF_ROWS)
     small[1].wait()
     a_roll[:, 512:WIN] = jnp.zeros((RANK, WIN - 512), F32)
@@ -230,6 +165,66 @@
             a_roll[...] = pltpu.roll(a_roll[...], offsets[quarter], axis=1)
     z_in[z] = a_roll[rank_rows, :].astype(BF16)
 
+    small[2].wait()
+    lw_t[...] = jnp.broadcast_to(lw_ref[...].astype(F32), (ROWS, ROWS)).T
+    pl.semaphore_wait(barrier, len(peers))
+
+    def doc_copy(j):
+        return push(doc_buf.at[own], doc_buf.at[own - j], doc_send.at[j - 1],
+                    doc_recv.at[own - j], (dp, c + j))
+
+    def kv_copy(h, kind, source, target, peer):
+        return push(kv_buf.at[h, source], kv_buf.at[h, target], send_sem.at[h, kind],
+                    recv_sem.at[h, target], (dp, peer))
+
+    def hop_own(h):
+        return kv_copy(h, 0, 4, 2, c + 2)
+
+    def pair_own(h):
+        return kv_copy(h, 1, 4, 3, c + 1)
+
+    def hop_relay(h):
+        return kv_copy(h, 2, 2, 0, c + 2)
+
+    def pair_near_up(h):
+        return kv_copy(h, 3, 2, 1, c + 1)
+
+    def pair_near_down(h):
+        return kv_copy(h, 3, 2, 3, c - 1)
+
+    def pair_far_down(h):
+        return kv_copy(h, 4, 0, 1, c - 1)
+
+    def back_own(h):
+        return push(kv_buf.at[h, own], back_buf.at[h], send_sem.at[h, 5], back_recv.at[h],
+                    (dp, ahead(c, 6, 8)))
+
+    def back_relay(h):
+        return push(back_buf.at[h], kv_buf.at[h, 0], send_sem.at[h, 6], recv_sem.at[h, 0],
+                    (dp, ahead(c, 6, 8)))
+
+    def is_back(h):
+        return h % 2 == 1
+
+    outer = jnp.logical_or(y == 0, y == 3)
+
+    def send_own(h, carry):
+        kv_load(h, 0).wait()
+        kv_load(h, 1).wait()
+
+        @pl.when(y < 3)
+        def _():
+            hop_own(h).start()
+
+        @pl.when(core == 0)
+        def _():
+            pair_own(h).start()
+
+        @pl.when(jnp.logical_and(is_back(h), y < 2))
+        def _():
+            back_own(h).start()
+        return carry
+
     span = (slice(0, 16), slice(16, 32))
 
     def fz_push(src, d, part):
@@ -237,9 +232,17 @@
                     fz_send.at[part, d - 1], fz_recv.at[part, d - 1],
                     at(x, ahead(z, d, NZ), y, core))
 
-    for part in range(2):
-        for d in (4, 3, 5, 2, 6, 1, 7):
-            fz_push(z, d, part).start()
+    for d in (4, 3, 5, 2, 6, 1, 7):
+        fz_push(z, d, 0).start()
+    send_own(0, 0)
+    for j in range(1, BLOCKS):
+        @pl.when(c + j < 8)
+        def _():
+            doc_copy(j).start()
+    send_own(1, 0)
+    for d in (4, 3, 5, 2, 6, 1, 7):
+        fz_push(z, d, 1).start()
+
 
     def section(xx):
         return pl.ds(pl.multiple_of(xx * XCOLS, HEAD), XCOLS)
@@ -338,8 +341,6 @@
         def _():
             pair_far_down(h).wait_recv()
 
-    small[2].wait()
-    lw_t[...] = jnp.broadcast_to(lw_ref[...].astype(F32), (ROWS, ROWS)).T
 
     relay_near(0)
     send_own(2, 0)

time: 71.4 us -> 71.4 us (level)
  no operation moved by 1% of the time
where the time goes in v5:
time: 71.4 us; the launch traced here: 71.3 us
  Pallas kernels  68.8 us (96%)
  other arithmetic  1.74 us (2%)
    pallas_call x1, Pallas kernels, reduced_gradient(): pl.pallas_call(kernel, out_shape=jax.ShapeDtypeStruct((RANK, 640), F32),...  68.8 us
    div x1, other arithmetic, per_device(): new_m / corr_one / (jnp.sqrt(new_v / corr_two) + ADAM_EPS)  1.74 us

profile of v5, /device:TPU:1, one launch (start us, length us, event | category | flops | bytes accessed | tf_op | source)
XLA Modules:
  0.0 71.3 jit_solution(14218428637011091159)
XLA Ops:
  0.6 0.0 copy-start
  0.6 0.0 copy-start.1
  0.7 68.8 %layer_back.1 = f32[64,640]{1,0:T(8,128)} custom-call(bf16[128,8192]{1,0:T(8,128)(2,1)} %bitcast.5, bf16[128,8192]{1,0:T(8,128)(2,1)} %bitcast.6, s32[1,128]{1,0:T(1,128)} %lw_hbm.1, s32[1,128]{1,0:T(1,128)} %docs_hbm.1, bf16[128,1024]{1,0:T(8,128)(2,1)} %bitcast.8, bf16[128,1024]{1,0:T(8,128)(2,1)} %bitcast.9, bf16[128,5120]{1,0:T(8,128)(2,1)} %bitcast.7, ...), custom_call_target="tpu_custom_call" | custom-call | flops 6006243328 | bytes 10000000 | tf_op jit(solution)/shard_map/layer_back/pallas_call | solution.py:723
  69.5 0.0 copy-done
  69.5 0.0 copy-done.1
  69.5 1.7 %add_divide_fusion = (f32[64,608]{1,0:T(8,128)}, f32[64,608]{1,0:T(8,128)}, f32[64,608]{1,0:T(8,128)}) fusion(f32[64,640]{1,0:T(8,128)} %layer_back.1, f32[64,608]{1,0:T(8,128)S(1)} %copy-done, f32[64,608]{1,0:T(8,128)S(1)} %copy-done.1), kind=kLoop, calls=%fused_computation.2 | loop fusion | flops 428032 | bytes 933888 | tf_op jit(solution)/shard_map/div | solution.py:772
Async XLA Ops:
  0.6 68.9 %copy-start = (f32[64,608]{1,0:T(8,128)S(1)}, f32[64,608]{1,0:T(8,128)}, u32[]{:S(2)}) copy-start(f32[64,608]{1,0:T(8,128)} %param.20) | copy-start | bytes 466948
  0.6 68.9 %copy-start.1 = (f32[64,608]{1,0:T(8,128)S(1)}, f32[64,608]{1,0:T(8,128)}, u32[]{:S(2)}) copy-start(f32[64,608]{1,0:T(8,128)} %param.19) | copy-start | bytes 466948
